TPU v7x, 32 devices: a whole 2x2x4 slice. The times are simulated.
32 devices in a mesh: row: 4 (over x, core), col: 8 (over z, y).
Axes of the slice: x: 2, y: 2, z: 4, core: 2. Of those that a mesh axis runs over, the one named last changes fastest.
Arguments:
- factors_u: bfloat16 [128, 1024, 128], P('row', 'col'), may hold values from -6 to 6
- covariates: bfloat16 [128, 1024, 512], P('row', 'col'), may hold values from -6 to 6
- link_beta: float32 [512, 128], replicated, may hold values from -0.25 to 0.25
- factors_v: float32 [4096, 128], P(('row', 'col')), may hold values from -0.5 to 0.5
- obs_values: bfloat16 [32, 128, 128, 128], P(('row', 'col')), may hold values from -6 to 6
- obs_blocks: int32 [32, 128], P(('row', 'col')), may hold values from 0 to 1023, as said below
- obs_count: int32 [32], P(('row', 'col')), may hold values from 1 to 128, as said below
- noise_u: bfloat16 [128, 1024, 128], P('row', 'col'), may hold values from -5 to 5
- noise_v: float32 [4096, 128], P(('row', 'col')), may hold values from -5 to 5
- noise_beta: float32 [512, 128], replicated, may hold values from -5 to 5
Outputs:
- u_next: bfloat16 [128, 1024, 128], P('row', 'col')
- v_next: float32 [4096, 128], P(('row', 'col'))
- beta_next: float32 [512, 128], replicated
Inputs may be any that keep to these rules, and one draw needn't show every extreme that they name: `obs_blocks`: A device's entries are distinct numbers pb * 32 + db with pb below 32. `obs_count`: some device's count is 128 in every draw.
All inputs are finite; a program needn't handle non-finite values.
Results may differ from a plain program's by a relative error of at most 0.0095.
Values may be sent and summed in bfloat16 or wider, within the bound.
A program may use at most 64 MiB of HBM per device.

v0:
```python
import math

import jax
import jax.numpy as jnp
from jax import lax
from jax.sharding import PartitionSpec as P

edge_weight = 0.5
ridge_weight = 0.1
step_pixel = 0.2


def with_halo(cells, sides, width):
    for axis, dim in sides:
        count = lax.axis_size(axis)
        ends = count - 1
        head = lax.slice_in_dim(cells, 0, width, axis=dim)
        tail = lax.slice_in_dim(cells, cells.shape[dim] - width, cells.shape[dim], axis=dim)
        cells = jnp.concatenate(
            [
                lax.ppermute(tail, axis, [(i, (i + 1) % count) for i in range(ends)]),
                cells,
                lax.ppermute(head, axis, [((i + 1) % count, i) for i in range(ends)]),
            ],
            axis=dim,
        )
    return cells


def split_sum(onehot, values):
    high = values.astype(jnp.bfloat16)
    rest = values - high.astype(jnp.float32)
    middle = rest.astype(jnp.bfloat16)
    lowest = (rest - middle.astype(jnp.float32)).astype(jnp.bfloat16)
    total = jnp.einsum("ps,pk->sk", onehot, high, preferred_element_type=jnp.float32)
    total = total + jnp.einsum("ps,pk->sk", onehot, middle, preferred_element_type=jnp.float32)
    return total + jnp.einsum("ps,pk->sk", onehot, lowest, preferred_element_type=jnp.float32)


def block_terms(u_rows, y_vals, pixel_ids, day_ids, live_count, day_table, tile_rows):
    slot_count, block_len, factor_rank = u_rows.shape
    day_blocks = day_table.shape[0]
    group_size = min(32, slot_count)
    turn_count = (live_count + group_size - 1) // group_size

    def one_turn(turn_index, carried):
        data_u, data_v = carried
        offset = turn_index * group_size
        u_part = lax.dynamic_slice_in_dim(u_rows, offset, group_size, 0)
        y_part = lax.dynamic_slice_in_dim(y_vals, offset, group_size, 0)
        d_part = lax.dynamic_slice_in_dim(day_ids, offset, group_size, 0)
        p_part = lax.dynamic_slice_in_dim(pixel_ids, offset, group_size, 0)
        v_part = day_table[d_part]
        predicted = jnp.einsum("pbk,pdk->pbd", u_part, v_part, preferred_element_type=jnp.float32)
        is_live = offset + jnp.arange(group_size) < live_count
        residual = jnp.where(
            is_live[:, None, None], y_part.astype(jnp.float32) - predicted, 0.0
        ).astype(jnp.bfloat16)
        grad_rows = jnp.einsum("pbd,pdk->pbk", residual, v_part, preferred_element_type=jnp.float32)
        day_terms = jnp.einsum("pbd,pbk->pdk", residual, u_part, preferred_element_type=jnp.float32)
        day_onehot = (d_part[:, None] == jnp.arange(day_blocks)[None, :]).astype(jnp.bfloat16)
        pixel_onehot = (p_part[:, None] == jnp.arange(tile_rows)[None, :]).astype(jnp.bfloat16)
        data_v = data_v + split_sum(day_onehot, day_terms.reshape(group_size, -1))
        data_u = data_u + split_sum(pixel_onehot, grad_rows.reshape(group_size, -1))
        return (data_u, data_v)

    initial = (
        jnp.zeros((tile_rows, block_len * factor_rank), jnp.float32),
        jnp.zeros((day_blocks, block_len * factor_rank), jnp.float32),
    )
    return lax.fori_loop(0, turn_count, one_turn, initial)


def shards(
    factors_u,
    covariates,
    link_beta,
    factors_v,
    obs_values,
    obs_blocks,
    obs_count,
    noise_u,
    noise_v,
    noise_beta,
):
    row_count = lax.axis_size("row")
    col_count = lax.axis_size("col")
    device_count = row_count * col_count
    tile_rows, block_len, factor_rank = factors_u.shape
    covar_count = covariates.shape[2]
    own_days = factors_v.astype(jnp.bfloat16)
    day_flat = lax.all_gather(own_days, ("row", "col"), axis=0, tiled=True)
    total_days = day_flat.shape[0]
    day_blocks = total_days // block_len
    day_table = day_flat.reshape(day_blocks, block_len, factor_rank)
    beta_bf = link_beta.astype(jnp.bfloat16)
    covar_rows = covariates.reshape(-1, covar_count)
    mean_field = jnp.dot(covar_rows, beta_bf, preferred_element_type=jnp.float32).reshape(
        tile_rows, block_len, factor_rank
    )
    resid_field = factors_u.astype(jnp.float32) - mean_field
    padded = with_halo(resid_field.astype(jnp.bfloat16), (("row", 0), ("col", 1)), 1).astype(
        resid_field.dtype
    )
    laplace = 4.0 * resid_field - (
        padded[2:, 1:-1] + padded[:-2, 1:-1] + padded[1:-1, 2:] + padded[1:-1, :-2]
    )
    prior_pull = edge_weight * laplace + ridge_weight * resid_field
    prior_bf = prior_pull.astype(jnp.bfloat16)
    link_part = lax.dot_general(
        covar_rows,
        prior_bf.reshape(-1, factor_rank),
        (((0,), (0,)), ((), ())),
        preferred_element_type=jnp.float32,
    )
    link_grad = lax.psum(link_part, ("row", "col"))
    blocks = obs_blocks[0]
    slot_count = blocks.shape[0]
    pixel_ids = blocks // day_blocks
    day_ids = blocks % day_blocks
    u_rows = factors_u[pixel_ids]
    data_flat, day_sums = block_terms(
        u_rows, obs_values[0], pixel_ids, day_ids, obs_count[0], day_table, tile_rows
    )
    data_u = data_flat.reshape(tile_rows, block_len, factor_rank)
    day_terms = day_sums.reshape(total_days, factor_rank)
    per_device = total_days // device_count
    arranged = (
        day_terms.reshape(row_count, col_count, per_device, factor_rank)
        .transpose(1, 0, 2, 3)
        .reshape(total_days, factor_rank)
    )
    data_v = lax.psum_scatter(
        lax.psum_scatter(
            arranged.astype(jnp.bfloat16), "col", scatter_dimension=0, tiled=True
        ).astype(jnp.float32),
        "row",
        scatter_dimension=0,
        tiled=True,
    )
    u_next = (
        factors_u.astype(jnp.float32)
        + 0.5 * step_pixel * (data_u - prior_pull)
        + math.sqrt(step_pixel) * noise_u.astype(jnp.float32)
    ).astype(jnp.bfloat16)
    step_day = 0.25 / math.sqrt(device_count * slot_count * block_len / day_blocks)
    v_next = factors_v + 0.5 * step_day * (data_v - factors_v) + math.sqrt(step_day) * noise_v
    step_link = 0.25 / math.sqrt(device_count * tile_rows * block_len)
    beta_next = (
        link_beta + 0.5 * step_link * (link_grad - link_beta) + math.sqrt(step_link) * noise_beta
    )
    return (u_next, v_next, beta_next)


def solution(mesh):
    in_specs = (
        P("row", "col", None),
        P("row", "col", None),
        P(),
        P(("row", "col"), None),
        P(("row", "col"), None, None, None),
        P(("row", "col"), None),
        P(("row", "col")),
        P("row", "col", None),
        P(("row", "col"), None),
        P(),
    )
    out_specs = (P("row", "col", None), P(("row", "col"), None), P())
    return jax.shard_map(shards, mesh=mesh, in_specs=in_specs, out_specs=out_specs, check_vma=False)
```

profile of v0, /device:TPU:0, one launch (start us, length us, event | category | flops | bytes accessed | tf_op | source)
XLA Modules:
  0.0 369.2 jit_solution(7307620179743235331)
XLA Ops:
  10.1 4.3 %gather_fusion.1 = bf16[128,128,128]{2,1,0:T(8,128)(2,1)} fusion(bf16[32,128,128]{2,1,0:T(8,128)(2,1)} %param.12, s32[1024]{0:T(1024)S(1)} %pad_clamp_fusion.1), kind=kCustom, calls=%fused_computation.1 | custom fusion | bytes 8389120 | tf_op jit(solution)/shard_map/gather | solution.py:121
  14.4 53.8 %all-gather.2.cloned.1.call-done = bf16[4096,128]{1,0:T(8,128)(2,1)} async-done(((bf16[128,128]{1,0:T(8,128)(2,1)}), bf16[4096,128]{1,0:T(8,128)(2,1)}) %all-gather.2.cloned.1.call-update) | async-done | bytes 1048592 | tf_op jit(solution)/shard_map/all_gather | solution.py:92
  69.8 73.5 %while.12 = (s32[]{:T(128)}, f32[32,16384]{1,0:T(8,128)S(1)}, f32[32,16384]{1,0:T(8,128)}, s32[]{:T(128)}, s32[128]{0:T(128)S(1)}, /*index=5*/s32[]{:T(128)}, bf...) while((s32[]{:T(128)}, f32[32,16384]{1,0:T(8,128)S(1)}, ...), condition=%wide.region_1.2_spmd, body=%wide.region_0.0_spmd.sunk | while | flops 620764288 | bytes 69213128 | solution.py:71
  69.9 2.0 gather_fusion
  72.5 2.4 select_convert_fusion.2
  80.2 1.8 fusion.65
  85.1 1.8 fusion.67
  88.3 2.0 gather_fusion
  90.9 2.4 select_convert_fusion.2
  98.6 1.8 fusion.65
  103.5 1.8 fusion.67
  106.7 2.0 gather_fusion
  109.3 2.4 select_convert_fusion.2
  117.0 1.8 fusion.65
  125.0 2.0 gather_fusion
  127.7 2.4 select_convert_fusion.2
  135.4 1.8 fusion.65
  146.6 3.4 fusion.31
  151.4 3.0 collective-permute-start
  156.6 4.5 %collective-permute-start.2 = (bf16[34,1,128]{2,1,0:T(2,128)(2,1)S(1)}, bf16[34,1,128]{2,1,0:T(2,128)(2,1)S(1)}, u32[]{:S(2)}, u32[]{:S(2)}) collective-permute-start(bf16[34,1,128]{2,1,0:T(2,128)(2,1)S(1)} %get-tuple-element.86), channel_id=1, source_target_pairs={{0,1},{1,2},{2,3},{3,4},{4,5},{5,6},{6,7},{8,9},{9,10},{10,11},{11... | collective-permute-start | bytes 26120 | tf_op jit(solution)/shard_map/ppermute | solution.py:21
  164.2 2.6 fusion.20
  168.3 40.4 %reduce-scatter.3.cloned.1.call-done = bf16[512,128]{1,0:T(8,128)(2,1)} async-done(((bf16[4096,128]{1,0:T(8,128)(2,1)}), bf16[512,128]{1,0:T(8,128)(2,1)}) %reduce-scatter.3.cloned.1.call-update) | async-done | bytes 131088 | tf_op jit(solution)/shard_map/reduce_scatter | solution.py:134
  210.7 129.0 %all-reduce.2.cloned.1.call-done = f32[512,128]{0,1:T(8,128)} async-done(((f32[512,128]{0,1:T(8,128)}), f32[512,128]{0,1:T(8,128)}) %all-reduce.2.cloned.1.call-update) | async-done | bytes 262160 | tf_op jit(solution)/shard_map/psum | solution.py:116
  341.6 19.7 %reduce-scatter.5.cloned.1.call-done = f32[128,128]{1,0:T(8,128)} async-done(((f32[512,128]{1,0:T(8,128)}), f32[128,128]{1,0:T(8,128)}) %reduce-scatter.5.cloned.1.call-update) | async-done | bytes 65552 | tf_op jit(solution)/shard_map/reduce_scatter | solution.py:133
  (107 shorter events, 65.6 us)
Async XLA Ops:
  7.2 61.0 %all-gather.2.cloned.1.call-start = ((), (), s32[]{:S(2)}) async-start(), calls=%async_computation.2 | async-start | bytes 1081344 | tf_op jit(solution)/shard_map/all_gather | solution.py:92
  8.7 200.0 %reduce-scatter.3.cloned.1.call-start = ((), (), s32[]{:S(2)}) async-start(), calls=%async_computation.3 | async-start | bytes 1179648 | tf_op jit(solution)/shard_map/reduce_scatter | solution.py:134
  10.1 4.3 %copy-start.9 = (s32[1,128]{1,0:T(1,128)S(1)}, s32[1,128]{1,0:T(1,128)}, u32[]{:S(2)}) copy-start(s32[1,128]{1,0:T(1,128)} %param.17) | copy-start | bytes 1540
  83.5 1.6 copy-start
  86.9 1.3 copy-start.1
  101.9 1.6 copy-start
  105.2 1.3 copy-start.1
  120.3 1.6 copy-start
  123.6 1.3 copy-start.1
  138.7 1.6 copy-start
  142.0 1.3 copy-start.1
  145.1 1.5 copy-start.2
  145.1 1.5 copy-start.5
  146.4 193.3 %all-reduce.2.cloned.1.call-start = ((), (), s32[]{:S(2)}) async-start(), calls=%async_computation.5 | async-start | bytes 524288 | tf_op jit(solution)/shard_map/psum | solution.py:116
  150.1 4.3 %collective-permute-start.1 = (bf16[1,128,128]{2,1,0:T(8,128)(2,1)S(1)}, bf16[1,128,128]{2,1,0:T(8,128)(2,1)S(1)}, u32[]{:S(2)}, u32[]{:S(2)}) collective-permute-start(bf16[1,128,128]{2,1,0:T(8,128)(2,1)S(1)} %get-tuple-element.89), channel_id=1, source_target_pairs={{8,0},{16,8},{24,16},{9,1},{17,9},{25,17},{10,2},{18,10},{26,18},{... | collective-permute-start | bytes 98312 | tf_op jit(solution)/shard_map/ppermute | solution.py:23
  151.4 3.9 %collective-permute-start = (bf16[1,128,128]{2,1,0:T(8,128)(2,1)S(1)}, bf16[1,128,128]{2,1,0:T(8,128)(2,1)S(1)}, u32[]{:S(2)}, u32[]{:S(2)}) collective-permute-start(bf16[1,128,128]{2,1,0:T(8,128)(2,1)S(1)} %get-tuple-element.88), channel_id=1, source_target_pairs={{0,8},{8,16},{16,24},{1,9},{9,17},{17,25},{2,10},{10,18},{18,26},{... | collective-permute-start | bytes 98312 | tf_op jit(solution)/shard_map/ppermute | solution.py:21
  155.3 5.9 %collective-permute-start.3 = (bf16[34,1,128]{2,1,0:T(2,128)(2,1)S(1)}, bf16[34,1,128]{2,1,0:T(2,128)(2,1)S(1)}, u32[]{:S(2)}, u32[]{:S(2)}) collective-permute-start(bf16[34,1,128]{2,1,0:T(2,128)(2,1)S(1)} %get-tuple-element.87), channel_id=1, source_target_pairs={{1,0},{2,1},{3,2},{4,3},{5,4},{6,5},{7,6},{9,8},{10,9},{11,10},{12... | collective-permute-start | bytes 26120 | tf_op jit(solution)/shard_map/ppermute | solution.py:23
  156.6 6.0 %collective-permute-start.2 = (bf16[34,1,128]{2,1,0:T(2,128)(2,1)S(1)}, bf16[34,1,128]{2,1,0:T(2,128)(2,1)S(1)}, u32[]{:S(2)}, u32[]{:S(2)}) collective-permute-start(bf16[34,1,128]{2,1,0:T(2,128)(2,1)S(1)} %get-tuple-element.86), channel_id=1, source_target_pairs={{0,1},{1,2},{2,3},{3,4},{4,5},{5,6},{6,7},{8,9},{9,10},{10,11},{11... | collective-permute-start | bytes 26120 | tf_op jit(solution)/shard_map/ppermute | solution.py:21
  163.0 1.2 copy-start.4
  164.2 2.6 copy-start.3
  166.8 43.8 %copy-start.6 = (f32[512,128]{1,0:T(8,128)S(1)}, f32[512,128]{1,0:T(8,128)}, u32[]{:S(2)}) copy-start(f32[512,128]{1,0:T(8,128)} %param.21) | copy-start | bytes 786436
  168.2 193.0 %copy-start.7 = (f32[128,128]{1,0:T(8,128)S(1)}, f32[128,128]{1,0:T(8,128)}, u32[]{:S(2)}) copy-start(f32[128,128]{1,0:T(8,128)} %param.15) | copy-start | bytes 196612
  168.2 193.0 %copy-start.8 = (f32[128,128]{1,0:T(8,128)S(1)}, f32[128,128]{1,0:T(8,128)}, u32[]{:S(2)}) copy-start(f32[128,128]{1,0:T(8,128)} %param.20) | copy-start | bytes 196612
  168.3 193.0 %reduce-scatter.5.cloned.1.call-start = ((), (), s32[]{:S(2)}) async-start(), calls=%async_computation.4 | async-start | bytes 327680 | tf_op jit(solution)/shard_map/reduce_scatter | solution.py:133
Sparse Core Ops, SparseCore 0:
  11.6 56.5 all-gather.1
  146.5 62.1 reduce-scatter.2
  215.7 123.9 all-reduce.1
  342.2 19.0 reduce-scatter.4
where the time goes:
time: 370 us; the launch traced here: 369 us
  waiting for transfers between devices  245 us (66%)
  matrix products  61.4 us (17%)
  local copies, waits for them, and re-layouts  23.2 us (6%)
  between operations  14.6 us (4%)
  other arithmetic  13.9 us (4%)
  starting transfers between devices  10.5 us (3%)
    psum x1, waiting for transfers between devices, shards(): link_grad = lax.psum(link_part, ('row', 'col'))  129 us
    all_gather x1, waiting for transfers between devices, shards(): day_flat = lax.all_gather(own_days, ('row', 'col'), axis=0, tiled=True)  53.8 us
    reduce_scatter x1, waiting for transfers between devices, shards(): lax.psum_scatter(arranged.astype(jnp.bfloat16), 'col', scatter_dimension=...  40.4 us
    reduce_scatter x1, waiting for transfers between devices, shards(): lax.psum_scatter(lax.psum_scatter(arranged.astype(jnp.bfloat16), 'col', s...  19.7 us
    dot_general x8, matrix products, split_sum(): jnp.einsum('ps,pk->sk', onehot, lowest, preferred_element_type=jnp.float32)  14 us
    dot_general x8, matrix products, split_sum(): jnp.einsum('ps,pk->sk', onehot, middle, preferred_element_type=jnp.float32)  12.2 us
    dot_general x8, matrix products, split_sum(): jnp.einsum('ps,pk->sk', onehot, high, preferred_element_type=jnp.float32)  11.9 us
    dot_general x4, matrix products, one_turn(): jnp.einsum('pbk,pdk->pbd', u_part, v_part, preferred_element_type=jnp.flo...  9.55 us
  transfers between devices with their start and end apart: 8, of which 6 were waited for; matrix products, arithmetic and copies ran while one was open for 5% of the time, Pallas kernels for 0%

commit v1 on v0

v1 whole, which is shorter than its diff:
```python
import functools
import math

import jax
import jax.numpy as jnp
from jax import lax
from jax.experimental import pallas as pl
from jax.experimental.pallas import tpu as pltpu
from jax.sharding import PartitionSpec as P

edge_weight = 0.5
ridge_weight = 0.1
step_pixel = 0.2
MESH = pl.DeviceIdType.MESH
F32 = jnp.float32
BF16 = jnp.bfloat16
VMEM = pl.BlockSpec(memory_space=pltpu.VMEM)
ANY = pl.BlockSpec(memory_space=pl.ANY)
LIMIT = 48 * 1024 * 1024


class Place:
    def __init__(self, rows, cols):
        self.rows, self.cols = rows, cols
        self.nr, self.nc = rows // 2, cols // 2
        self.r, self.c = lax.axis_index("row"), lax.axis_index("col")
        self.r1, self.r0 = self.r // 2, lax.rem(self.r, 2)
        self.c1, self.c0 = self.c // 2, lax.rem(self.c, 2)
        self.core = (self.r1 * 2 + (1 - self.r0), self.c)
        self.side = (self.r, self.c1 * 2 + (1 - self.c0))

    def r1_at(self, k):
        return lax.rem(self.r1 + k, self.nr)

    def c1_at(self, k):
        return lax.rem(self.c1 + k, self.nc)

    def x_peer(self, k):
        return (self.r1_at(k) * 2 + self.r0, self.c)

    def z_peer(self, k):
        return (self.r, self.c1_at(k) * 2 + self.c0)

    def partners(self):
        return (
            [self.core, self.side]
            + [self.x_peer(k) for k in range(1, self.nr)]
            + [self.z_peer(k) for k in range(1, self.nc)]
        )


def greet(partners):
    barrier = pltpu.get_barrier_semaphore()
    for partner in partners:
        pl.semaphore_signal(barrier, inc=1, device_id=partner, device_id_type=MESH)
    pl.semaphore_wait(barrier, len(partners))


def send(src, dst, send_sem, recv_sem, device):
    copy = pltpu.make_async_remote_copy(
        src_ref=src, dst_ref=dst, send_sem=send_sem, recv_sem=recv_sem,
        device_id=device, device_id_type=MESH,
    )
    copy.start()
    return copy


def field_kernel(
    rows, cols, fv_ref, beta_ref, cov_hbm, u_hbm, nz_hbm,
    days, base_ref, link_ref,
    cov, u, nz, beta, rp, edge_send, edge_recv, link_acc,
    load_sem, day_send, day_recv, halo_send, halo_recv,
):
    at = Place(rows, cols)
    nr, nc = at.nr, at.nc
    tile, block = u.shape[0], u.shape[1]
    parts = 4
    per = tile // parts
    loads = []
    for k in range(parts):
        loads.append(pltpu.make_async_copy(cov_hbm.at[pl.ds(k * per, per)], cov.at[pl.ds(k * per, per)], load_sem.at[k]))
    u_load = pltpu.make_async_copy(u_hbm, u, load_sem.at[parts])
    nz_load = pltpu.make_async_copy(nz_hbm, nz, load_sem.at[parts + 1])
    loads[0].start()
    u_load.start()
    for load in loads[1:]:
        load.start()
    nz_load.start()

    days[at.r1, at.r0, at.c1, at.c0] = fv_ref[...].astype(BF16)
    north = (lax.rem(at.r + rows - 1, rows), at.c)
    south = (lax.rem(at.r + 1, rows), at.c)
    west = (at.r, lax.rem(at.c + cols - 1, cols))
    east = (at.r, lax.rem(at.c + 1, cols))
    greet(at.partners() + [north, south, west, east])

    sends = []

    def block_at(b):
        return days.at[b[0], b[1], b[2], b[3]]

    def sem_at(b):
        return day_recv.at[((b[0] * 2 + b[1]) * nc + b[2]) * 2 + b[3]]

    def pass_on(b, partners):
        for partner in partners:
            sends.append(send(block_at(b), block_at(b), day_send.at[len(sends)], sem_at(b), partner))

    def arrive(b):
        pltpu.make_async_remote_copy(
            src_ref=block_at(b), dst_ref=block_at(b), send_sem=day_send.at[0], recv_sem=sem_at(b),
            device_id=at.core, device_id_type=MESH,
        ).wait_recv()

    zs = [at.z_peer(k) for k in range(1, nc)]
    xs = [at.x_peer(k) for k in range(1, nr)]
    own = (at.r1, at.r0, at.c1, at.c0)
    pass_on(own, zs + [at.side] + xs + [at.core])

    beta[...] = beta_ref[...].astype(BF16)

    def resid_rows(i):
        cells = cov[pl.ds(i, per)].reshape(per * block, cov.shape[2])
        mean = jnp.dot(cells, beta[...], preferred_element_type=F32)
        rp[pl.ds(i + 1, per)] = u[pl.ds(i, per)].astype(F32) - mean.reshape(per, block, -1)

    u_load.wait()
    for k in range(parts):
        loads[k].wait()
        resid_rows(k * per)
    edge_send[0] = rp[pl.ds(1, tile), 0, :]
    edge_send[1] = rp[pl.ds(1, tile), block - 1, :]
    halos = [
        send(rp.at[1], rp.at[tile + 1], halo_send.at[0], halo_recv.at[0], north),
        send(rp.at[tile], rp.at[0], halo_send.at[1], halo_recv.at[1], south),
        send(edge_send.at[0], edge_recv.at[1], halo_send.at[2], halo_recv.at[2], west),
        send(edge_send.at[1], edge_recv.at[0], halo_send.at[3], halo_recv.at[3], east),
    ]

    for k in range(1, nc):
        b = (at.r1, at.r0, at.c1_at(nc - k), at.c0)
        arrive(b)
        pass_on(b, [at.side] + xs + [at.core])
    for k in range(nc):
        b = (at.r1, at.r0, at.c1_at(nc - k), 1 - at.c0)
        arrive(b)
        pass_on(b, xs + [at.core])

    nz_load.wait()
    for halo in halos:
        halo.wait()
    for spot, gone in ((0, at.r == 0), (tile + 1, at.r == rows - 1)):
        rp[spot] = jnp.where(gone, 0.0, rp[spot])
    for spot, gone in ((0, at.c == 0), (1, at.c == cols - 1)):
        edge_recv[spot] = jnp.where(gone, 0.0, edge_recv[spot])

    lane_row = lax.broadcasted_iota(jnp.int32, (per, block, u.shape[2]), 1)

    def prior_rows(i):
        mid = rp[pl.ds(i + 1, per)]
        around = rp[pl.ds(i, per)] + rp[pl.ds(i + 2, per)]
        left = jnp.where(lane_row == 0, edge_recv[0, pl.ds(i, per)][:, None, :], pltpu.roll(mid, 1, 1))
        right = jnp.where(
            lane_row == block - 1, edge_recv[1, pl.ds(i, per)][:, None, :], pltpu.roll(mid, block - 1, 1)
        )
        laplace = 4.0 * mid - (around + right + left)
        prior = edge_weight * laplace + ridge_weight * mid
        base_ref[pl.ds(i, per)] = (
            u[pl.ds(i, per)].astype(F32)
            - 0.5 * step_pixel * prior
            + math.sqrt(step_pixel) * nz[pl.ds(i, per)].astype(F32)
        )
        return lax.dot_general(
            prior.astype(BF16).reshape(per * block, -1),
            cov[pl.ds(i, per)].reshape(per * block, cov.shape[2]),
            (((0,), (0,)), ((), ())),
            preferred_element_type=F32,
        )

    for k in range(parts):
        if k == 0:
            link_acc[...] = prior_rows(0)
        else:
            link_acc[...] += prior_rows(k * per)

    for j in range(1, nr):
        for k in range(nc):
            for c0 in (at.c0, 1 - at.c0):
                b = (at.r1_at(nr - j), at.r0, at.c1_at(nc - k), c0)
                arrive(b)
                pass_on(b, [at.core])
    link_ref[...] = link_acc[...].T
    for j in range(nr):
        for k in range(nc):
            for c0 in (at.c0, 1 - at.c0):
                arrive((at.r1_at(nr - j), 1 - at.r0, at.c1_at(nc - k), c0))
    for copy in sends:
        copy.wait_send()


def run_field(rows, cols, factors_v, link_beta, covariates, factors_u, noise_u):
    tile, block, rank = factors_u.shape
    covar = covariates.shape[2]
    per_device = factors_v.shape[0]
    count = rows * cols
    return pl.pallas_call(
        functools.partial(field_kernel, rows, cols),
        out_shape=(
            jax.ShapeDtypeStruct((rows // 2, 2, cols // 2, 2, per_device, rank), BF16),
            jax.ShapeDtypeStruct((tile, block, rank), F32),
            jax.ShapeDtypeStruct((covar, rank), F32),
        ),
        in_specs=[VMEM, VMEM, ANY, ANY, ANY],
        out_specs=(VMEM, VMEM, VMEM),
        scratch_shapes=[
            pltpu.VMEM((tile, block, covar), BF16),
            pltpu.VMEM((tile, block, rank), BF16),
            pltpu.VMEM((tile, block, rank), BF16),
            pltpu.VMEM((covar, rank), BF16),
            pltpu.VMEM((tile + 2, block, rank), F32),
            pltpu.VMEM((2, tile, rank), F32),
            pltpu.VMEM((2, tile, rank), F32),
            pltpu.VMEM((rank, covar), F32),
            pltpu.SemaphoreType.DMA((6,)),
            pltpu.SemaphoreType.DMA((count,)),
            pltpu.SemaphoreType.DMA((count,)),
            pltpu.SemaphoreType.DMA((4,)),
            pltpu.SemaphoreType.DMA((4,)),
        ],
        compiler_params=pltpu.CompilerParams(
            collective_id=0, has_side_effects=True, vmem_limit_bytes=LIMIT
        ),
    )(factors_v, link_beta, covariates, factors_u, noise_u)


def slots_kernel(group, blocks_ref, count_ref, obs_ref, u_ref, v_ref, base_ref, next_ref, dv_ref, acc_u, acc_v):
    step = pl.program_id(0)
    day_blocks = v_ref.shape[0]

    @pl.when(step == 0)
    def _():
        acc_u[...] = base_ref[...]
        acc_v[...] = jnp.zeros_like(acc_v)

    live = count_ref[0]
    wide = 4

    def turn(t, carry):
        found = []
        for j in range(wide):
            s = t * wide + j
            slot = step * group + s
            e = blocks_ref[slot]
            pb, db = e // day_blocks, lax.rem(e, day_blocks)
            uu, vv = u_ref[pb], v_ref[db]
            predicted = lax.dot_general(uu, vv, (((1,), (1,)), ((), ())), preferred_element_type=F32)
            residual = jnp.where(slot < live, obs_ref[s].astype(F32) - predicted, 0.0).astype(BF16)
            grad = jnp.dot(residual, vv, preferred_element_type=F32)
            day = lax.dot_general(residual, uu, (((0,), (0,)), ((), ())), preferred_element_type=F32)
            found.append((pb, db, grad, day))
        for pb, db, grad, day in found:
            acc_u[pb] += 0.5 * step_pixel * grad
            acc_v[db] += day
        return carry

    lax.fori_loop(0, group // wide, turn, 0)

    @pl.when(step == pl.num_programs(0) - 1)
    def _():
        next_ref[...] = acc_u[...].astype(BF16)
        dv_ref[...] = acc_v[...].astype(BF16)


def run_slots(blocks, live, obs, factors_u, day_table, base):
    slots, block, _ = obs.shape
    tile, _, rank = factors_u.shape
    day_blocks = day_table.shape[0]
    group = 16
    whole = lambda shape: pl.BlockSpec(shape, lambda i, *_: (0,) * len(shape))
    return pl.pallas_call(
        functools.partial(slots_kernel, group),
        out_shape=(
            jax.ShapeDtypeStruct((tile, block, rank), BF16),
            jax.ShapeDtypeStruct((day_blocks, block, rank), BF16),
        ),
        grid_spec=pltpu.PrefetchScalarGridSpec(
            num_scalar_prefetch=2,
            grid=(slots // group,),
            in_specs=[
                pl.BlockSpec((group, block, block), lambda i, *_: (i, 0, 0)),
                whole(factors_u.shape),
                whole(day_table.shape),
                whole(base.shape),
            ],
            out_specs=(whole((tile, block, rank)), whole((day_blocks, block, rank))),
            scratch_shapes=[
                pltpu.VMEM((tile, block, rank), F32),
                pltpu.VMEM((day_blocks, block, rank), F32),
            ],
        ),
        compiler_params=pltpu.CompilerParams(vmem_limit_bytes=LIMIT),
    )(blocks, live, obs, factors_u, day_table, base)


def sum_kernel(
    rows, cols, step_day, step_link,
    dv, lk, fv_ref, nv_ref, beta_ref, nb_ref,
    v_ref, beta_out,
    got_core, mid_core, got_x, mid_x, got_side, mid_side, got_z,
    lk_core, lm_core, lk_x, lm_x, lk_side, lk_z, total,
    send_sem, recv_sem,
):
    at = Place(rows, cols)
    nr, nc = at.nr, at.nc
    greet(at.partners())
    used = [0]
    pending = []

    def post(src, dst, device):
        k = used[0]
        used[0] += 1
        copy = send(src, dst, send_sem.at[k], recv_sem.at[k], device)
        pending.append(copy)
        return copy

    def settle(copies):
        for copy in copies:
            copy.wait_recv()

    a = [post(dv.at[:, 1 - at.r0], got_core, at.core)]
    b = [post(lk.at[1 - at.r0], lk_core, at.core)]
    settle(a)
    mid_core[...] = (dv[:, at.r0].astype(F32) + got_core[...].astype(F32)).astype(BF16)
    a = [post(mid_core.at[at.r1_at(k)], got_x.at[k - 1], at.x_peer(k)) for k in range(1, nr)]
    settle(b)
    lm_core[...] = lk[at.r0] + lk_core[...]
    b = [post(lm_core.at[at.r1_at(k)], lk_x.at[k - 1], at.x_peer(k)) for k in range(1, nr)]
    settle(a)
    part = mid_core[at.r1].astype(F32)
    for k in range(nr - 1):
        part = part + got_x[k].astype(F32)
    mid_x[...] = part.astype(BF16)
    a = [post(mid_x.at[:, 1 - at.c0], got_side, at.side)]
    settle(b)
    link = lm_core[at.r1]
    for k in range(nr - 1):
        link = link + lk_x[k]
    lm_x[...] = link
    b = [post(lm_x.at[1 - at.c0], lk_side, at.side)]
    settle(a)
    mid_side[...] = (mid_x[:, at.c0].astype(F32) + got_side[...].astype(F32)).astype(BF16)
    a = [post(mid_side.at[at.c1_at(k)], got_z.at[k - 1], at.z_peer(k)) for k in range(1, nc)]
    settle(b)
    lk_z[at.c1] = lm_x[at.c0] + lk_side[...]
    b = [post(lk_z.at[at.c1], lk_z.at[at.c1], at.z_peer(k)) for k in range(1, nc)]
    settle(b)
    link = lk_z[0]
    for k in range(1, nc):
        link = link + lk_z[k]
    total[at.r0, at.r1, at.c0] = link
    b = [post(total.at[at.r0, at.r1, at.c0], total.at[at.r0, at.r1, at.c0], at.side)]
    settle(a)
    part = mid_side[at.c1].astype(F32)
    for k in range(nc - 1):
        part = part + got_z[k].astype(F32)
    old = fv_ref[...]
    v_ref[...] = old + 0.5 * step_day * (part - old) + math.sqrt(step_day) * nv_ref[...]
    settle(b)
    b = [post(total.at[at.r0, at.r1], total.at[at.r0, at.r1], at.x_peer(k)) for k in range(1, nr)]
    settle(b)
    b = [post(total.at[at.r0], total.at[at.r0], at.core)]
    settle(b)
    old = beta_ref[...]
    beta_out[...] = old + 0.5 * step_link * (total[...] - old) + math.sqrt(step_link) * nb_ref[...]
    for copy in pending:
        copy.wait_send()


def run_sum(rows, cols, step_day, step_link, dv, link_part, factors_v, noise_v, link_beta, noise_beta):
    nr, nc = rows // 2, cols // 2
    per_device, rank = factors_v.shape
    covar = link_beta.shape[0]
    piece = covar // (4 * nr)
    lshape = (2, nr, 2, piece, rank)
    sends = 2 * (1 + (nr - 1) + 1 + (nc - 1)) + 1 + (nr - 1) + 1
    v_next, beta_next = pl.pallas_call(
        functools.partial(sum_kernel, rows, cols, step_day, step_link),
        out_shape=(
            jax.ShapeDtypeStruct((per_device, rank), F32),
            jax.ShapeDtypeStruct(lshape, F32),
        ),
        in_specs=[VMEM] * 6,
        out_specs=(VMEM, VMEM),
        scratch_shapes=[
            pltpu.VMEM((nr, nc, 2, per_device, rank), BF16),
            pltpu.VMEM((nr, nc, 2, per_device, rank), BF16),
            pltpu.VMEM((nr - 1, nc, 2, per_device, rank), BF16),
            pltpu.VMEM((nc, 2, per_device, rank), BF16),
            pltpu.VMEM((nc, per_device, rank), BF16),
            pltpu.VMEM((nc, per_device, rank), BF16),
            pltpu.VMEM((nc - 1, per_device, rank), BF16),
            pltpu.VMEM((nr, 2, piece, rank), F32),
            pltpu.VMEM((nr, 2, piece, rank), F32),
            pltpu.VMEM((nr - 1, 2, piece, rank), F32),
            pltpu.VMEM((2, piece, rank), F32),
            pltpu.VMEM((piece, rank), F32),
            pltpu.VMEM((nc, piece, rank), F32),
            pltpu.VMEM(lshape, F32),
            pltpu.SemaphoreType.DMA((sends,)),
            pltpu.SemaphoreType.DMA((sends,)),
        ],
        compiler_params=pltpu.CompilerParams(
            collective_id=1, has_side_effects=True, vmem_limit_bytes=LIMIT
        ),
    )(
        dv.reshape(nr, 2, nc, 2, per_device, rank),
        link_part.reshape(lshape),
        factors_v,
        noise_v,
        link_beta.reshape(lshape),
        noise_beta.reshape(lshape),
    )
    return v_next, beta_next.reshape(covar, rank)


def shards(
    factors_u, covariates, link_beta, factors_v, obs_values, obs_blocks, obs_count,
    noise_u, noise_v, noise_beta,
):
    rows = lax.axis_size("row")
    cols = lax.axis_size("col")
    devices = rows * cols
    tile, block, rank = factors_u.shape
    per_device = factors_v.shape[0]
    days = per_device * devices
    day_blocks = days // block
    slots = obs_blocks.shape[1]
    day_table, base, link_part = run_field(
        rows, cols, factors_v, link_beta, covariates, factors_u, noise_u
    )
    u_next, dv = run_slots(
        obs_blocks[0], obs_count, obs_values[0], factors_u,
        day_table.reshape(day_blocks, block, rank), base,
    )
    step_day = 0.25 / math.sqrt(devices * slots * block / day_blocks)
    step_link = 0.25 / math.sqrt(devices * tile * block)
    v_next, beta_next = run_sum(
        rows, cols, step_day, step_link, dv, link_part, factors_v, noise_v, link_beta, noise_beta
    )
    return (u_next, v_next, beta_next)


def solution(mesh):
    in_specs = (
        P("row", "col", None),
        P("row", "col", None),
        P(),
        P(("row", "col"), None),
        P(("row", "col"), None, None, None),
        P(("row", "col"), None),
        P(("row", "col")),
        P("row", "col", None),
        P(("row", "col"), None),
        P(),
    )
    out_specs = (P("row", "col", None), P(("row", "col"), None), P())
    return jax.shard_map(shards, mesh=mesh, in_specs=in_specs, out_specs=out_specs, check_vma=False)
```

time: 370 us -> 73.4 us (0.20)
  waiting for transfers between devices: 245 us -> 0 us
  Pallas kernels: 0 us -> 66.2 us
  matrix products: 61.4 us -> 0 us
  local copies, waits for them, and re-layouts: 23.2 us -> 5.59 us
  other arithmetic: 13.9 us -> 0 us
  between operations: 14.6 us -> 1.36 us
  starting transfers between devices: 10.5 us -> 0 us
    psum x1 -> x0, waiting for transfers between devices: 129 us -> none  [shards(): link_grad = lax.psum(link_part, ('row', 'col'))]
    pallas_call x0 -> x3, Pallas kernels: none -> 66.2 us  [the longest x1 29.6 us: run_sum(): pl.pallas_call(functools.partial(sum_kernel, rows, cols, step_day, step_l...]
    dot_general x38 -> x0, matrix products: 61.4 us -> none  [the longest x8 14 us: split_sum(): jnp.einsum('ps,pk->sk', onehot, lowest, preferred_element_type=jnp.float32)]
    reduce_scatter x2 -> x0, waiting for transfers between devices: 60.1 us -> none  [the longest x1 40.4 us: shards(): lax.psum_scatter(arranged.astype(jnp.bfloat16), 'col', scatter_dimension=...]
    all_gather x1 -> x0, waiting for transfers between devices: 53.8 us -> none  [shards(): day_flat = lax.all_gather(own_days, ('row', 'col'), axis=0, tiled=True)]
    gather x5 -> x0, local copies, waits for them, and re-layouts: 12.1 us -> none  [the longest x4 7.88 us: one_turn(): v_part = day_table[d_part]]
    ppermute x4 -> x0, starting transfers between devices: 10.2 us -> none  [the longest x2 7.58 us: with_halo(): lax.ppermute(tail, axis, [(i, (i + 1) % count) for i in range(ends)])]
    convert_element_type x5 -> x0, other arithmetic: 7.77 us -> none  [the longest x1 2.56 us: shards(): u_next = (factors_u.astype(jnp.float32) + 0.5 * step_pixel * (data_u - pr...]
  transfers between devices with their start and end apart: 8 -> 0, of which waited for: 6 -> 0; matrix products, arithmetic and copies ran while one was open for 5% -> 0% of each run, Pallas kernels for 0% -> 0%
where the time goes in v1:
time: 73.4 us; the launch traced here: 73.1 us
  Pallas kernels  66.2 us (90%)
  local copies, waits for them, and re-layouts  5.59 us (8%)
  between operations  1.36 us (2%)
    pallas_call x1, Pallas kernels, run_sum(): pl.pallas_call(functools.partial(sum_kernel, rows, cols, step_day, step_l...  29.6 us
    pallas_call x1, Pallas kernels, run_field(): pl.pallas_call(functools.partial(field_kernel, rows, cols), out_shape=(ja...  18.8 us
    pallas_call x1, Pallas kernels, run_slots(): pl.pallas_call(functools.partial(slots_kernel, group), out_shape=(jax.Sha...  17.8 us
    unnamed x18, local copies, waits for them, and re-layouts  5.59 us

profile of v1, /device:TPU:0, one launch (start us, length us, event | category | flops | bytes accessed | tf_op | source)
XLA Modules:
  0.0 73.1 jit_solution(14655377950976182399)
XLA Ops:
  0.6 0.0 copy-start.7
  1.3 0.0 copy-start
  1.3 1.2 %copy-done = bf16[32,128,128]{2,1,0:T(8,128)(2,1)S(1)} copy-done((bf16[32,128,128]{2,1,0:T(8,128)(2,1)S(1)}, bf16[32,128,128]{2,1,0:T(8,128)(2,1)}, u32[]{:S(2)}) %copy-start) | copy-done | bytes 1048600
  2.5 0.0 copy-start.2
  2.5 1.2 %copy-done.2 = bf16[32,128,128]{2,1,0:T(8,128)(2,1)S(1)} copy-done((bf16[32,128,128]{2,1,0:T(8,128)(2,1)S(1)}, bf16[32,128,128]{2,1,0:T(8,128)(2,1)}, u32[]{:S(2)}) %copy-start.2) | copy-done | bytes 1048600
  3.8 0.0 copy-start.3
  3.8 0.9 %copy-done.3 = f32[512,128]{1,0:T(8,128)S(1)} copy-done((f32[512,128]{1,0:T(8,128)S(1)}, f32[512,128]{1,0:T(8,128)}, u32[]{:S(2)}) %copy-start.3) | copy-done | bytes 262168
  4.7 0.0 copy-start.4
  4.7 0.8 %copy-done.4 = f32[128,128]{1,0:T(8,128)S(1)} copy-done((f32[128,128]{1,0:T(8,128)S(1)}, f32[128,128]{1,0:T(8,128)}, u32[]{:S(2)}) %copy-start.4) | copy-done | bytes 65560
  5.5 0.0 copy-start.1
  5.5 18.8 %shard_map.121 = (bf16[2,2,4,2,128,128]{5,4,3,2,1,0:T(8,128)(2,1)S(1)}, f32[32,128,128]{2,1,0:T(8,128)S(1)}, f32[512,128]{1,0:T(8,128)S(1)}) custom-call(f32[128,128]{1,0:T(8,128)S(1)} %copy-done.4, f32[512,128]{1,0:T(8,128)S(1)} %copy-done.3, bf16[32,128,512]{2,1,0:T(8,128)(2,1)} %cov_hbm.1, bf16[32,128,128]{2,1,0:T(8,128)(2,1)S(1)} %copy-done, ...), custom_call_target="tpu_custom_call" | custom-call | tf_op jit(solution)/shard_map/pallas_call | solution.py:206
  24.4 0.0 copy-done.7
  24.4 0.0 copy-done.1
  24.4 0.0 copy-start.5
  24.4 0.0 copy-start.6
  24.4 17.8 %shard_map.122 = (bf16[32,128,128]{2,1,0:T(8,128)(2,1)}, bf16[32,128,128]{2,1,0:T(8,128)(2,1)S(1)}) custom-call(s32[128]{0:T(128)S(1)} %bitcast.14, s32[1]{0:T(128)S(6)} %copy.15.count_ref, bf16[128,128,128]{2,1,0:T(8,128)(2,1)} %bitcast.15, bf16[32,128,128]{2,1,0:T(8,128)(2,1)S(1)} %copy-done.1, bf16[32,128,128]{2,1,0:T(8,128)(2,1)S(1)} %bitcast.8, ...), custom_call_target="tpu_custom_call" | custom-call | tf_op jit(solution)/shard_map/pallas_call | solution.py:280
  42.2 0.0 copy-done.5
  42.2 0.0 copy-done.6
  42.2 29.6 %shard_map.123 = (f32[128,128]{1,0:T(8,128)S(1)}, f32[2,2,2,64,128]{4,3,2,1,0:T(8,128)S(1)}) custom-call(bf16[2,2,4,2,128,128]{5,4,3,2,1,0:T(8,128)(2,1)S(1)} %bitcast.10, f32[2,2,2,64,128]{4,3,2,1,0:T(8,128)S(1)} %bitcast.12, f32[128,128]{1,0:T(8,128)S(1)} %copy-done.4, f32[128,128]{1,0:T(8,128)S(1)} %copy-done.6, f32[2,2,2,64,128]{4,3,2,1,0:T(8,128)S(1)} %bitcast.9, ...), custom_call_target="tpu_custom_call" | custom-call | tf_op jit(solution)/shard_map/pallas_call | solution.py:386
  71.8 0.6 copy.16
  72.4 0.7 copy.17
Async XLA Ops:
  0.6 23.7 %copy-start.7 = (s32[1,128]{1,0:T(1,128)S(1)}, s32[1,128]{1,0:T(1,128)}, u32[]{:S(2)}) copy-start(s32[1,128]{1,0:T(1,128)} %param.15) | copy-start | bytes 1540
  1.3 1.2 %copy-start = (bf16[32,128,128]{2,1,0:T(8,128)(2,1)S(1)}, bf16[32,128,128]{2,1,0:T(8,128)(2,1)}, u32[]{:S(2)}) copy-start(bf16[32,128,128]{2,1,0:T(8,128)(2,1)} %u_ref.1) | copy-start | bytes 3145732
  2.5 1.2 %copy-start.2 = (bf16[32,128,128]{2,1,0:T(8,128)(2,1)S(1)}, bf16[32,128,128]{2,1,0:T(8,128)(2,1)}, u32[]{:S(2)}) copy-start(bf16[32,128,128]{2,1,0:T(8,128)(2,1)} %nz_hbm.1) | copy-start | bytes 3145732
  3.8 0.9 %copy-start.3 = (f32[512,128]{1,0:T(8,128)S(1)}, f32[512,128]{1,0:T(8,128)}, u32[]{:S(2)}) copy-start(f32[512,128]{1,0:T(8,128)} %beta_ref.1) | copy-start | bytes 786436
  4.7 0.8 %copy-start.4 = (f32[128,128]{1,0:T(8,128)S(1)}, f32[128,128]{1,0:T(8,128)}, u32[]{:S(2)}) copy-start(f32[128,128]{1,0:T(8,128)} %fv_ref.3) | copy-start | bytes 196612
  5.5 18.8 %copy-start.1 = (bf16[32,128,128]{2,1,0:T(8,128)(2,1)S(1)}, bf16[32,128,128]{2,1,0:T(8,128)(2,1)}, u32[]{:S(2)}) copy-start(bf16[32,128,128]{2,1,0:T(8,128)(2,1)} %u_ref.1) | copy-start | bytes 3145732
  24.4 17.8 %copy-start.5 = (f32[512,128]{1,0:T(8,128)S(1)}, f32[512,128]{1,0:T(8,128)}, u32[]{:S(2)}) copy-start(f32[512,128]{1,0:T(8,128)} %param.19) | copy-start | bytes 786436
  24.4 17.8 %copy-start.6 = (f32[128,128]{1,0:T(8,128)S(1)}, f32[128,128]{1,0:T(8,128)}, u32[]{:S(2)}) copy-start(f32[128,128]{1,0:T(8,128)} %nv_ref.1) | copy-start | bytes 196612

commit v2 on v1

v2 whole, which is shorter than its diff:
```python
import functools
import math

import jax
import jax.numpy as jnp
from jax import lax
from jax.experimental import pallas as pl
from jax.experimental.pallas import tpu as pltpu
from jax.sharding import PartitionSpec as P

edge_weight = 0.5
ridge_weight = 0.1
step_pixel = 0.2
MESH = pl.DeviceIdType.MESH
F32 = jnp.float32
BF16 = jnp.bfloat16
VMEM = pl.BlockSpec(memory_space=pltpu.VMEM)
ANY = pl.BlockSpec(memory_space=pl.ANY)
LIMIT = 40 * 1024 * 1024


class Place:
    def __init__(self, rows, cols):
        self.rows, self.cols = rows, cols
        self.nr, self.nc = rows // 2, cols // 2
        self.r, self.c = lax.axis_index("row"), lax.axis_index("col")
        self.r1, self.r0 = self.r // 2, lax.rem(self.r, 2)
        self.c1, self.c0 = self.c // 2, lax.rem(self.c, 2)
        self.core = (self.r1 * 2 + (1 - self.r0), self.c)
        self.side = (self.r, self.c1 * 2 + (1 - self.c0))

    def r1_at(self, k):
        return lax.rem(self.r1 + k, self.nr)

    def c1_at(self, k):
        return lax.rem(self.c1 + k, self.nc)

    def x_peer(self, k):
        return (self.r1_at(k) * 2 + self.r0, self.c)

    def z_peer(self, k):
        return (self.r, self.c1_at(k) * 2 + self.c0)

    def partners(self):
        return (
            [self.core, self.side]
            + [self.x_peer(k) for k in range(1, self.nr)]
            + [self.z_peer(k) for k in range(1, self.nc)]
        )


def greet(partners):
    barrier = pltpu.get_barrier_semaphore()
    for partner in partners:
        pl.semaphore_signal(barrier, inc=1, device_id=partner, device_id_type=MESH)
    pl.semaphore_wait(barrier, len(partners))


def send(src, dst, send_sem, recv_sem, device):
    copy = pltpu.make_async_remote_copy(
        src_ref=src, dst_ref=dst, send_sem=send_sem, recv_sem=recv_sem,
        device_id=device, device_id_type=MESH,
    )
    copy.start()
    return copy


def field_kernel(
    rows, cols, blocks_ref, live_ref, fv_ref, beta_ref, cov_hbm, u_hbm, nz_hbm, obs_hbm,
    base_ref, total, grad_ref, term_ref,
    days, cov, u, nz, obs, beta, rp, edge_send, edge_recv, link_acc,
    lk, lk_core, lm_core, lk_x, lm_x, lk_side, lk_z,
    load_sem, day_send, day_recv, halo_send, halo_recv, link_send, link_recv,
):
    at = Place(rows, cols)
    nr, nc = at.nr, at.nc
    tile, block = u.shape[0], u.shape[1]
    parts = 4
    per = tile // parts
    loads = []
    for k in range(parts):
        loads.append(pltpu.make_async_copy(cov_hbm.at[pl.ds(k * per, per)], cov.at[pl.ds(k * per, per)], load_sem.at[k]))
    u_load = pltpu.make_async_copy(u_hbm, u, load_sem.at[parts])
    nz_load = pltpu.make_async_copy(nz_hbm, nz, load_sem.at[parts + 1])
    loads[0].start()
    u_load.start()
    for load in loads[1:]:
        load.start()
    nz_load.start()
    obs_load = pltpu.make_async_copy(obs_hbm, obs, load_sem.at[parts + 2])
    obs_load.start()

    def index_of(b):
        return ((b[0] * 2 + b[1]) * nc + b[2]) * 2 + b[3]

    days[at.r * cols + at.c] = fv_ref[...].astype(BF16)
    north = (lax.rem(at.r + rows - 1, rows), at.c)
    south = (lax.rem(at.r + 1, rows), at.c)
    west = (at.r, lax.rem(at.c + cols - 1, cols))
    east = (at.r, lax.rem(at.c + 1, cols))
    greet(at.partners() + [north, south, west, east])

    sends = []

    def block_at(b):
        return days.at[index_of(b)]

    def sem_at(b):
        return day_recv.at[index_of(b)]

    def pass_on(b, partners):
        for partner in partners:
            sends.append(send(block_at(b), block_at(b), day_send.at[len(sends)], sem_at(b), partner))

    def arrive(b):
        pltpu.make_async_remote_copy(
            src_ref=block_at(b), dst_ref=block_at(b), send_sem=day_send.at[0], recv_sem=sem_at(b),
            device_id=at.core, device_id_type=MESH,
        ).wait_recv()

    zs = [at.z_peer(k) for k in range(1, nc)]
    xs = [at.x_peer(k) for k in range(1, nr)]
    own = (at.r1, at.r0, at.c1, at.c0)
    pass_on(own, zs + [at.side] + xs + [at.core])

    beta[...] = beta_ref[...].astype(BF16)

    def resid_rows(i):
        cells = cov[pl.ds(i, per)].reshape(per * block, cov.shape[2])
        mean = jnp.dot(cells, beta[...], preferred_element_type=F32)
        rp[pl.ds(i + 1, per)] = u[pl.ds(i, per)].astype(F32) - mean.reshape(per, block, -1)

    u_load.wait()
    for k in range(parts):
        loads[k].wait()
        resid_rows(k * per)
    edge_send[0] = rp[pl.ds(1, tile), 0, :]
    edge_send[1] = rp[pl.ds(1, tile), block - 1, :]
    halos = [
        send(rp.at[1], rp.at[tile + 1], halo_send.at[0], halo_recv.at[0], north),
        send(rp.at[tile], rp.at[0], halo_send.at[1], halo_recv.at[1], south),
        send(edge_send.at[0], edge_recv.at[1], halo_send.at[2], halo_recv.at[2], west),
        send(edge_send.at[1], edge_recv.at[0], halo_send.at[3], halo_recv.at[3], east),
    ]

    for k in range(1, nc):
        b = (at.r1, at.r0, at.c1_at(nc - k), at.c0)
        arrive(b)
        pass_on(b, [at.side] + xs + [at.core])
    for k in range(nc):
        b = (at.r1, at.r0, at.c1_at(nc - k), 1 - at.c0)
        arrive(b)
        pass_on(b, xs + [at.core])

    nz_load.wait()
    for halo in halos:
        halo.wait()
    for spot, gone in ((0, at.r == 0), (tile + 1, at.r == rows - 1)):
        rp[spot] = jnp.where(gone, 0.0, rp[spot])
    for spot, gone in ((0, at.c == 0), (1, at.c == cols - 1)):
        edge_recv[spot] = jnp.where(gone, 0.0, edge_recv[spot])

    lane_row = lax.broadcasted_iota(jnp.int32, (per, block, u.shape[2]), 1)

    def prior_rows(i):
        mid = rp[pl.ds(i + 1, per)]
        around = rp[pl.ds(i, per)] + rp[pl.ds(i + 2, per)]
        left = jnp.where(lane_row == 0, edge_recv[0, pl.ds(i, per)][:, None, :], pltpu.roll(mid, 1, 1))
        right = jnp.where(
            lane_row == block - 1, edge_recv[1, pl.ds(i, per)][:, None, :], pltpu.roll(mid, block - 1, 1)
        )
        laplace = 4.0 * mid - (around + right + left)
        prior = edge_weight * laplace + ridge_weight * mid
        base_ref[pl.ds(i, per)] = (
            u[pl.ds(i, per)].astype(F32)
            - 0.5 * step_pixel * prior
            + math.sqrt(step_pixel) * nz[pl.ds(i, per)].astype(F32)
        )
        return lax.dot_general(
            prior.astype(BF16).reshape(per * block, -1),
            cov[pl.ds(i, per)].reshape(per * block, cov.shape[2]),
            (((0,), (0,)), ((), ())),
            preferred_element_type=F32,
        )

    for k in range(parts):
        if k == 0:
            link_acc[...] = prior_rows(0)
        else:
            link_acc[...] += prior_rows(k * per)

    for j in range(1, nr):
        for k in range(nc):
            for c0 in (at.c0, 1 - at.c0):
                b = (at.r1_at(nr - j), at.r0, at.c1_at(nc - k), c0)
                arrive(b)
                pass_on(b, [at.core])
    lk[...] = link_acc[...].T.reshape(lk.shape)
    used = [0]
    pending = []

    def post(src, dst, device):
        k = used[0]
        used[0] += 1
        copy = send(src, dst, link_send.at[k], link_recv.at[k], device)
        pending.append(copy)
        return copy

    def settle(copies):
        for copy in copies:
            copy.wait_recv()

    hop = [post(lk.at[1 - at.r0], lk_core, at.core)]
    for j in range(nr):
        for k in range(nc):
            for c0 in (at.c0, 1 - at.c0):
                arrive((at.r1_at(nr - j), 1 - at.r0, at.c1_at(nc - k), c0))
    obs_load.wait()

    live = live_ref[0]
    day_blocks = days.shape[0] * days.shape[1] // block
    span = block // days.shape[1]
    slots = obs.shape[0]
    wide = 4
    stages = 7
    turns = slots // wide

    def turn(t, carry):
        for j in range(wide):
            slot = t * wide + j
            e = blocks_ref[slot]
            pb, db = e // day_blocks, lax.rem(e, day_blocks)
            uu = u[pb]
            vv = days[pl.ds(db * span, span)].reshape(block, u.shape[2])
            predicted = lax.dot_general(uu, vv, (((1,), (1,)), ((), ())), preferred_element_type=F32)
            residual = jnp.where(slot < live, obs[slot].astype(F32) - predicted, 0.0).astype(BF16)
            grad_ref[slot] = jnp.dot(residual, vv, preferred_element_type=F32).astype(BF16)
            term_ref[slot] = lax.dot_general(
                residual, uu, (((0,), (0,)), ((), ())), preferred_element_type=F32
            ).astype(BF16)
        return carry

    for stage in range(stages + 1):
        lax.fori_loop(stage * turns // (stages + 1), (stage + 1) * turns // (stages + 1), turn, 0)
        settle(hop)
        if stage == 0:
            lm_core[...] = lk[at.r0] + lk_core[...]
            hop = [post(lm_core.at[at.r1_at(k)], lk_x.at[k - 1], at.x_peer(k)) for k in range(1, nr)]
        elif stage == 1:
            link = lm_core[at.r1]
            for k in range(nr - 1):
                link = link + lk_x[k]
            lm_x[...] = link
            hop = [post(lm_x.at[1 - at.c0], lk_side, at.side)]
        elif stage == 2:
            lk_z[at.c1] = lm_x[at.c0] + lk_side[...]
            hop = [post(lk_z.at[at.c1], lk_z.at[at.c1], at.z_peer(k)) for k in range(1, nc)]
        elif stage == 3:
            link = lk_z[0]
            for k in range(1, nc):
                link = link + lk_z[k]
            total[at.r0, at.r1, at.c0] = link
            hop = [post(total.at[at.r0, at.r1, at.c0], total.at[at.r0, at.r1, at.c0], at.side)]
        elif stage == 4:
            hop = [post(total.at[at.r0, at.r1], total.at[at.r0, at.r1], at.x_peer(k)) for k in range(1, nr)]
        elif stage == 5:
            hop = [post(total.at[at.r0], total.at[at.r0], at.core)]
        else:
            hop = []
    for copy in sends + pending:
        copy.wait_send()


def run_field(rows, cols, blocks, live, factors_v, link_beta, covariates, factors_u, noise_u, obs):
    tile, block, rank = factors_u.shape
    covar = covariates.shape[2]
    per_device = factors_v.shape[0]
    slots = obs.shape[0]
    count = rows * cols
    nr, nc = rows // 2, cols // 2
    piece = covar // (4 * nr)
    lshape = (2, nr, 2, piece, rank)
    hops = 2 * (1 + (nr - 1) + 1) + (nc - 1)
    smem = pl.BlockSpec(memory_space=pltpu.SMEM)
    return pl.pallas_call(
        functools.partial(field_kernel, rows, cols),
        out_shape=(
            jax.ShapeDtypeStruct((tile, block, rank), F32),
            jax.ShapeDtypeStruct(lshape, F32),
            jax.ShapeDtypeStruct((slots, block, rank), BF16),
            jax.ShapeDtypeStruct((slots, block, rank), BF16),
        ),
        in_specs=[smem, smem, VMEM, VMEM, ANY, ANY, ANY, ANY],
        out_specs=(VMEM, VMEM, VMEM, VMEM),
        scratch_shapes=[
            pltpu.VMEM((count, per_device, rank), BF16),
            pltpu.VMEM((tile, block, covar), BF16),
            pltpu.VMEM((tile, block, rank), BF16),
            pltpu.VMEM((tile, block, rank), BF16),
            pltpu.VMEM((slots, block, block), BF16),
            pltpu.VMEM((covar, rank), BF16),
            pltpu.VMEM((tile + 2, block, rank), F32),
            pltpu.VMEM((2, tile, rank), F32),
            pltpu.VMEM((2, tile, rank), F32),
            pltpu.VMEM((rank, covar), F32),
            pltpu.VMEM(lshape, F32),
            pltpu.VMEM((nr, 2, piece, rank), F32),
            pltpu.VMEM((nr, 2, piece, rank), F32),
            pltpu.VMEM((nr - 1, 2, piece, rank), F32),
            pltpu.VMEM((2, piece, rank), F32),
            pltpu.VMEM((piece, rank), F32),
            pltpu.VMEM((nc, piece, rank), F32),
            pltpu.SemaphoreType.DMA((7,)),
            pltpu.SemaphoreType.DMA((count,)),
            pltpu.SemaphoreType.DMA((count,)),
            pltpu.SemaphoreType.DMA((4,)),
            pltpu.SemaphoreType.DMA((4,)),
            pltpu.SemaphoreType.DMA((hops,)),
            pltpu.SemaphoreType.DMA((hops,)),
        ],
        compiler_params=pltpu.CompilerParams(
            collective_id=0, has_side_effects=True, vmem_limit_bytes=LIMIT
        ),
    )(blocks, live, factors_v, link_beta, covariates, factors_u, noise_u, obs)


def add_kernel(day_blocks, step_link, blocks_ref, base_ref, grad_ref, term_ref, total_ref, beta_ref, nb_ref,
               next_ref, dv_ref, beta_out, acc_u, acc_v):
    acc_u[...] = base_ref[...]
    acc_v[...] = jnp.zeros_like(acc_v)
    wide = 4

    def turn(t, carry):
        for j in range(wide):
            slot = t * wide + j
            e = blocks_ref[slot]
            pb, db = e // day_blocks, lax.rem(e, day_blocks)
            acc_u[pb] += 0.5 * step_pixel * grad_ref[slot].astype(F32)
            acc_v[db] += term_ref[slot].astype(F32)
        return carry

    lax.fori_loop(0, grad_ref.shape[0] // wide, turn, 0)
    next_ref[...] = acc_u[...].astype(BF16)
    dv_ref[...] = acc_v[...].astype(BF16)
    old = beta_ref[...]
    beta_out[...] = old + 0.5 * step_link * (total_ref[...] - old) + math.sqrt(step_link) * nb_ref[...]


def run_add(day_blocks, step_link, blocks, base, grad, term, total, link_beta, noise_beta):
    tile, block, rank = base.shape
    return pl.pallas_call(
        functools.partial(add_kernel, day_blocks, step_link),
        out_shape=(
            jax.ShapeDtypeStruct((tile, block, rank), BF16),
            jax.ShapeDtypeStruct((day_blocks, block, rank), BF16),
            jax.ShapeDtypeStruct(link_beta.shape, F32),
        ),
        in_specs=[pl.BlockSpec(memory_space=pltpu.SMEM)] + [VMEM] * 6,
        out_specs=(VMEM, VMEM, VMEM),
        scratch_shapes=[
            pltpu.VMEM((tile, block, rank), F32),
            pltpu.VMEM((day_blocks, block, rank), F32),
        ],
        compiler_params=pltpu.CompilerParams(vmem_limit_bytes=LIMIT),
    )(blocks, base, grad, term, total, link_beta, noise_beta)


def sum_kernel(
    rows, cols, step_day, dv, fv_ref, nv_ref, v_ref,
    got_a, got_b, mid_a, mid_b, far_a, far_b, part_a, part_b, last_a, last_b, mid, got_z,
    send_sem, recv_sem,
):
    at = Place(rows, cols)
    nr, nc = at.nr, at.nc
    half = nc // 2
    greet(at.partners())
    used = [0]
    pending = []

    def post(src, dst, device):
        k = used[0]
        used[0] += 1
        copy = send(src, dst, send_sem.at[k], recv_sem.at[k], device)
        pending.append(copy)
        return copy

    def settle(copies):
        for copy in copies:
            copy.wait_recv()

    def summed(own, refs):
        part = own.astype(F32)
        for ref in refs:
            part = part + ref.astype(F32)
        return part

    first, second = pl.ds(0, half), pl.ds(half, half)
    a = [post(dv.at[:, 1 - at.r0, first], got_a, at.core)]
    b = [post(dv.at[:, 1 - at.r0, second], got_b, at.core)]
    settle(a)
    mid_a[...] = summed(dv[:, at.r0, first], [got_a[...]]).astype(BF16)
    a = [post(mid_a.at[at.r1_at(k)], far_a.at[k - 1], at.x_peer(k)) for k in range(1, nr)]
    settle(b)
    mid_b[...] = summed(dv[:, at.r0, second], [got_b[...]]).astype(BF16)
    b = [post(mid_b.at[:, :, 1 - at.c0], far_b, at.side)]
    settle(a)
    part_a[...] = summed(mid_a[at.r1], [far_a[k] for k in range(nr - 1)]).astype(BF16)
    a = [post(part_a.at[:, 1 - at.c0], last_a, at.side)]
    settle(b)
    part_b[...] = summed(mid_b[:, :, at.c0], [far_b[...]]).astype(BF16)
    b = [post(part_b.at[at.r1_at(k)], last_b.at[k - 1], at.x_peer(k)) for k in range(1, nr)]
    settle(a)
    mid[first] = summed(part_a[:, at.c0], [last_a[...]]).astype(BF16)
    settle(b)
    mid[second] = summed(part_b[at.r1], [last_b[k] for k in range(nr - 1)]).astype(BF16)
    a = [post(mid.at[at.c1_at(k)], got_z.at[k - 1], at.z_peer(k)) for k in range(1, nc)]
    settle(a)
    part = summed(mid[at.c1], [got_z[k] for k in range(nc - 1)])
    old = fv_ref[...]
    v_ref[...] = old + 0.5 * step_day * (part - old) + math.sqrt(step_day) * nv_ref[...]
    for copy in pending:
        copy.wait_send()


def run_sum(rows, cols, step_day, dv, factors_v, noise_v):
    nr, nc = rows // 2, cols // 2
    half = nc // 2
    per_device, rank = factors_v.shape
    sends = 2 * (1 + (nr - 1) + 1) + (nc - 1)
    buf = lambda *lead: pltpu.VMEM((*lead, per_device, rank), BF16)
    return pl.pallas_call(
        functools.partial(sum_kernel, rows, cols, step_day),
        out_shape=jax.ShapeDtypeStruct((per_device, rank), F32),
        in_specs=[VMEM] * 3,
        out_specs=VMEM,
        scratch_shapes=[
            buf(nr, half, 2), buf(nr, half, 2),
            buf(nr, half, 2), buf(nr, half, 2),
            buf(nr - 1, half, 2), buf(nr, half),
            buf(half, 2), buf(nr, half),
            buf(half), buf(nr - 1, half),
            buf(nc), buf(nc - 1),
            pltpu.SemaphoreType.DMA((sends,)),
            pltpu.SemaphoreType.DMA((sends,)),
        ],
        compiler_params=pltpu.CompilerParams(
            collective_id=1, has_side_effects=True, vmem_limit_bytes=LIMIT
        ),
    )(dv.reshape(nr, 2, nc, 2, per_device, rank), factors_v, noise_v)


def shards(
    factors_u, covariates, link_beta, factors_v, obs_values, obs_blocks, obs_count,
    noise_u, noise_v, noise_beta,
):
    rows = lax.axis_size("row")
    cols = lax.axis_size("col")
    devices = rows * cols
    tile, block, rank = factors_u.shape
    per_device = factors_v.shape[0]
    days = per_device * devices
    day_blocks = days // block
    slots = obs_blocks.shape[1]
    step_day = 0.25 / math.sqrt(devices * slots * block / day_blocks)
    step_link = 0.25 / math.sqrt(devices * tile * block)
    base, total, grad, term = run_field(
        rows, cols, obs_blocks[0], obs_count, factors_v, link_beta, covariates, factors_u, noise_u,
        obs_values[0],
    )
    u_next, dv, beta_next = run_add(
        day_blocks, step_link, obs_blocks[0], base, grad, term,
        total.reshape(link_beta.shape), link_beta, noise_beta,
    )
    v_next = run_sum(rows, cols, step_day, dv, factors_v, noise_v)
    return (u_next, v_next, beta_next)


def solution(mesh):
    in_specs = (
        P("row", "col", None),
        P("row", "col", None),
        P(),
        P(("row", "col"), None),
        P(("row", "col"), None, None, None),
        P(("row", "col"), None),
        P(("row", "col")),
        P("row", "col", None),
        P(("row", "col"), None),
        P(),
    )
    out_specs = (P("row", "col", None), P(("row", "col"), None), P())
    return jax.shard_map(shards, mesh=mesh, in_specs=in_specs, out_specs=out_specs, check_vma=False)
```

time: 73.4 us -> 67.2 us (0.916)
  Pallas kernels: 66.2 us -> 60.1 us
    pallas_call x2, Pallas kernels: 47.4 us -> 19.3 us  [the longest x1 15.5 us: run_sum(): pl.pallas_call(functools.partial(sum_kernel, rows, cols, step_day), out_s...]
    pallas_call x1, Pallas kernels: 18.8 us -> 40.7 us  [run_field(): pl.pallas_call(functools.partial(field_kernel, rows, cols), out_shape=(ja...]
    unnamed x18 -> x15, local copies, waits for them, and re-layouts: 5.59 us -> 5.53 us
where the time goes in v2:
time: 67.2 us; the launch traced here: 66.9 us
  Pallas kernels  60.1 us (89%)
  local copies, waits for them, and re-layouts  5.53 us (8%)
  between operations  1.32 us (2%)
    pallas_call x1, Pallas kernels, run_field(): pl.pallas_call(functools.partial(field_kernel, rows, cols), out_shape=(ja...  40.7 us
    pallas_call x1, Pallas kernels, run_sum(): pl.pallas_call(functools.partial(sum_kernel, rows, cols, step_day), out_s...  15.5 us
    unnamed x15, local copies, waits for them, and re-layouts  5.53 us
    pallas_call x1, Pallas kernels, run_add(): pl.pallas_call(functools.partial(add_kernel, day_blocks, step_link), out_...  3.84 us

profile of v2, /device:TPU:0, one launch (start us, length us, event | category | flops | bytes accessed | tf_op | source)
XLA Modules:
  0.0 66.9 jit_solution(17776949693885401775)
XLA Ops:
  1.3 0.0 copy-start
  1.3 0.9 %copy-done = f32[512,128]{1,0:T(8,128)S(1)} copy-done((f32[512,128]{1,0:T(8,128)S(1)}, f32[512,128]{1,0:T(8,128)}, u32[]{:S(2)}) %copy-start) | copy-done | bytes 262168
  2.2 0.0 copy-start.1
  2.2 1.2 %copy-done.1 = bf16[32,128,128]{2,1,0:T(8,128)(2,1)S(1)} copy-done((bf16[32,128,128]{2,1,0:T(8,128)(2,1)S(1)}, bf16[32,128,128]{2,1,0:T(8,128)(2,1)}, u32[]{:S(2)}) %copy-start.1) | copy-done | bytes 1048600
  3.5 0.0 copy-start.2
  3.5 1.2 %copy-done.2 = bf16[32,128,128]{2,1,0:T(8,128)(2,1)S(1)} copy-done((bf16[32,128,128]{2,1,0:T(8,128)(2,1)S(1)}, bf16[32,128,128]{2,1,0:T(8,128)(2,1)}, u32[]{:S(2)}) %copy-start.2) | copy-done | bytes 1048600
  4.7 0.0 copy-start.3
  4.7 0.8 %copy-done.3 = f32[128,128]{1,0:T(8,128)S(1)} copy-done((f32[128,128]{1,0:T(8,128)S(1)}, f32[128,128]{1,0:T(8,128)}, u32[]{:S(2)}) %copy-start.3) | copy-done | bytes 65560
  5.5 0.0 copy-start.6
  5.5 0.7 copy-done.6
  6.2 0.0 copy-start.4
  6.2 40.7 %shard_map.121 = (f32[32,128,128]{2,1,0:T(8,128)S(1)}, f32[2,2,2,64,128]{4,3,2,1,0:T(8,128)S(1)}, bf16[128,128,128]{2,1,0:T(8,128)(2,1)S(1)}, bf16[128,128,128]{2,1,0:T(8,128)(2,1)S(1)}) custom-call(s32[128]{0:T(128)S(1)} %bitcast.6, s32[1]{0:T(128)S(6)} %copy.14.live_ref, f32[128,128]{1,0:T(8,128)S(1)} %copy-done.3, f32[512,128]{1,0:T(8,128)S(1)} %copy-done, ...), custom_call_target="tpu_custom_call" | custom-call | tf_op jit(solution)/shard_map/pallas_call | solution.py:285
  46.9 0.0 copy-done.4
  46.9 0.0 copy-start.5
  47.0 3.8 %shard_map.122 = (bf16[32,128,128]{2,1,0:T(8,128)(2,1)}, bf16[32,128,128]{2,1,0:T(8,128)(2,1)S(1)}, f32[512,128]{1,0:T(8,128)}) custom-call(s32[128]{0:T(128)S(1)} %bitcast.7, f32[32,128,128]{2,1,0:T(8,128)S(1)} %get-tuple-element.10.base_ref, bf16[128,128,128]{2,1,0:T(8,128)(2,1)S(1)} %get-tuple-element.11.grad_ref, ...), custom_call_target="tpu_custom_call" | custom-call | tf_op jit(solution)/shard_map/pallas_call | solution.py:351
  50.8 0.0 copy-done.5
  50.8 15.5 %shard_map.123 = f32[128,128]{1,0:T(8,128)S(1)} custom-call(bf16[2,2,4,2,128,128]{5,4,3,2,1,0:T(8,128)(2,1)S(1)} %bitcast.4, f32[128,128]{1,0:T(8,128)S(1)} %copy-done.3, f32[128,128]{1,0:T(8,128)S(1)} %copy-done.5), custom_call_target="tpu_custom_call" | custom-call | tf_op jit(solution)/shard_map/pallas_call | solution.py:431
  66.3 0.6 copy.15
Async XLA Ops:
  1.3 1.0 %copy-start = (f32[512,128]{1,0:T(8,128)S(1)}, f32[512,128]{1,0:T(8,128)}, u32[]{:S(2)}) copy-start(f32[512,128]{1,0:T(8,128)} %beta_ref.3) | copy-start | bytes 786436
  2.2 1.2 %copy-start.1 = (bf16[32,128,128]{2,1,0:T(8,128)(2,1)S(1)}, bf16[32,128,128]{2,1,0:T(8,128)(2,1)}, u32[]{:S(2)}) copy-start(bf16[32,128,128]{2,1,0:T(8,128)(2,1)} %u_hbm.1) | copy-start | bytes 3145732
  3.5 1.2 %copy-start.2 = (bf16[32,128,128]{2,1,0:T(8,128)(2,1)S(1)}, bf16[32,128,128]{2,1,0:T(8,128)(2,1)}, u32[]{:S(2)}) copy-start(bf16[32,128,128]{2,1,0:T(8,128)(2,1)} %nz_hbm.1) | copy-start | bytes 3145732
  4.7 0.8 %copy-start.3 = (f32[128,128]{1,0:T(8,128)S(1)}, f32[128,128]{1,0:T(8,128)}, u32[]{:S(2)}) copy-start(f32[128,128]{1,0:T(8,128)} %fv_ref.3) | copy-start | bytes 196612
  5.5 0.7 copy-start.6
  6.2 40.8 %copy-start.4 = (f32[512,128]{1,0:T(8,128)S(1)}, f32[512,128]{1,0:T(8,128)}, u32[]{:S(2)}) copy-start(f32[512,128]{1,0:T(8,128)} %nb_ref.1) | copy-start | bytes 786436
  46.9 3.9 %copy-start.5 = (f32[128,128]{1,0:T(8,128)S(1)}, f32[128,128]{1,0:T(8,128)}, u32[]{:S(2)}) copy-start(f32[128,128]{1,0:T(8,128)} %nv_ref.1) | copy-start | bytes 196612

commit v3 on v2

--- a/solution.py
+++ b/solution.py
@@ -15,8 +15,9 @@
 F32 = jnp.float32
 BF16 = jnp.bfloat16
 VMEM = pl.BlockSpec(memory_space=pltpu.VMEM)
-ANY = pl.BlockSpec(memory_space=pl.ANY)
+HBM = pl.BlockSpec(memory_space=pltpu.HBM)
 LIMIT = 40 * 1024 * 1024
+LIMIT_FIELD = 40 * 1024 * 1024
 
 
 class Place:
@@ -41,6 +42,15 @@
     def z_peer(self, k):
         return (self.r, self.c1_at(k) * 2 + self.c0)
 
+    def quad(self):
+        found = []
+        for k in range(self.nr):
+            for c0 in (self.c0, 1 - self.c0):
+                if k or c0 is not self.c0:
+                    r1 = self.r1_at(k)
+                    found.append(((r1 * 2 + self.r0, self.c1 * 2 + c0), r1, c0))
+        return found
+
     def partners(self):
         return (
             [self.core, self.side]
@@ -69,7 +79,7 @@
     rows, cols, blocks_ref, live_ref, fv_ref, beta_ref, cov_hbm, u_hbm, nz_hbm, obs_hbm,
     base_ref, total, grad_ref, term_ref,
     days, cov, u, nz, obs, beta, rp, edge_send, edge_recv, link_acc,
-    lk, lk_core, lm_core, lk_x, lm_x, lk_side, lk_z,
+    lk, lk_core, lm_core, lk_quad, lk_z, fv, beta_wide,
     load_sem, day_send, day_recv, halo_send, halo_recv, link_send, link_recv,
 ):
     at = Place(rows, cols)
@@ -82,6 +92,10 @@
         loads.append(pltpu.make_async_copy(cov_hbm.at[pl.ds(k * per, per)], cov.at[pl.ds(k * per, per)], load_sem.at[k]))
     u_load = pltpu.make_async_copy(u_hbm, u, load_sem.at[parts])
     nz_load = pltpu.make_async_copy(nz_hbm, nz, load_sem.at[parts + 1])
+    fv_load = pltpu.make_async_copy(fv_ref, fv, load_sem.at[parts + 3])
+    beta_load = pltpu.make_async_copy(beta_ref, beta_wide, load_sem.at[parts + 4])
+    fv_load.start()
+    beta_load.start()
     loads[0].start()
     u_load.start()
     for load in loads[1:]:
@@ -93,12 +107,17 @@
     def index_of(b):
         return ((b[0] * 2 + b[1]) * nc + b[2]) * 2 + b[3]
 
-    days[at.r * cols + at.c] = fv_ref[...].astype(BF16)
+    fv_load.wait()
+    days[at.r * cols + at.c] = fv[...].astype(BF16)
     north = (lax.rem(at.r + rows - 1, rows), at.c)
     south = (lax.rem(at.r + 1, rows), at.c)
     west = (at.r, lax.rem(at.c + cols - 1, cols))
     east = (at.r, lax.rem(at.c + 1, cols))
-    greet(at.partners() + [north, south, west, east])
+    quad = at.quad()
+    greet(
+        [at.core] + [q[0] for q in quad] + [at.z_peer(k) for k in range(1, nc)]
+        + [north, south, west, east]
+    )
 
     sends = []
 
@@ -123,7 +142,8 @@
     own = (at.r1, at.r0, at.c1, at.c0)
     pass_on(own, zs + [at.side] + xs + [at.core])
 
-    beta[...] = beta_ref[...].astype(BF16)
+    beta_load.wait()
+    beta[...] = beta_wide[...].astype(BF16)
 
     def resid_rows(i):
         cells = cov[pl.ds(i, per)].reshape(per * block, cov.shape[2])
@@ -221,23 +241,32 @@
     day_blocks = days.shape[0] * days.shape[1] // block
     span = block // days.shape[1]
     slots = obs.shape[0]
-    wide = 4
-    stages = 7
+    wide = 16
+    stages = 5
     turns = slots // wide
 
     def turn(t, carry):
+        taken = []
         for j in range(wide):
             slot = t * wide + j
             e = blocks_ref[slot]
             pb, db = e // day_blocks, lax.rem(e, day_blocks)
-            uu = u[pb]
-            vv = days[pl.ds(db * span, span)].reshape(block, u.shape[2])
+            taken.append((slot, u[pb], days[pl.ds(db * span, span)].reshape(block, u.shape[2]), obs[slot]))
+        resid = []
+        for slot, uu, vv, yy in taken:
             predicted = lax.dot_general(uu, vv, (((1,), (1,)), ((), ())), preferred_element_type=F32)
-            residual = jnp.where(slot < live, obs[slot].astype(F32) - predicted, 0.0).astype(BF16)
-            grad_ref[slot] = jnp.dot(residual, vv, preferred_element_type=F32).astype(BF16)
-            term_ref[slot] = lax.dot_general(
-                residual, uu, (((0,), (0,)), ((), ())), preferred_element_type=F32
-            ).astype(BF16)
+            resid.append(jnp.where(slot < live, yy.astype(F32) - predicted, 0.0).astype(BF16))
+        grads = [
+            jnp.dot(res, vv, preferred_element_type=F32).astype(BF16)
+            for res, (_, _, vv, _) in zip(resid, taken)
+        ]
+        terms = [
+            lax.dot_general(res, uu, (((0,), (0,)), ((), ())), preferred_element_type=F32).astype(BF16)
+            for res, (_, uu, _, _) in zip(resid, taken)
+        ]
+        for (slot, _, _, _), grad, term in zip(taken, grads, terms):
+            grad_ref[slot] = grad
+            term_ref[slot] = term
         return carry
 
     for stage in range(stages + 1):
@@ -245,25 +274,24 @@
         settle(hop)
         if stage == 0:
             lm_core[...] = lk[at.r0] + lk_core[...]
-            hop = [post(lm_core.at[at.r1_at(k)], lk_x.at[k - 1], at.x_peer(k)) for k in range(1, nr)]
+            hop = [
+                post(lm_core.at[r1, c0], lk_quad.at[q], device)
+                for q, (device, r1, c0) in enumerate(quad)
+            ]
         elif stage == 1:
-            link = lm_core[at.r1]
-            for k in range(nr - 1):
-                link = link + lk_x[k]
-            lm_x[...] = link
-            hop = [post(lm_x.at[1 - at.c0], lk_side, at.side)]
+            link = lm_core[at.r1, at.c0]
+            for q in range(len(quad)):
+                link = link + lk_quad[q]
+            lk_z[at.c1] = link
+            hop = [post(lk_z.at[at.c1], lk_z.at[at.c1], at.z_peer(k)) for k in range(1, nc)]
         elif stage == 2:
-            lk_z[at.c1] = lm_x[at.c0] + lk_side[...]
-            hop = [post(lk_z.at[at.c1], lk_z.at[at.c1], at.z_peer(k)) for k in range(1, nc)]
-        elif stage == 3:
             link = lk_z[0]
             for k in range(1, nc):
                 link = link + lk_z[k]
-            total[at.r0, at.r1, at.c0] = link
-            hop = [post(total.at[at.r0, at.r1, at.c0], total.at[at.r0, at.r1, at.c0], at.side)]
-        elif stage == 4:
-            hop = [post(total.at[at.r0, at.r1], total.at[at.r0, at.r1], at.x_peer(k)) for k in range(1, nr)]
-        elif stage == 5:
+            own_piece = total.at[at.r0, at.r1, at.c0]
+            own_piece[...] = link
+            hop = [post(own_piece, own_piece, device) for device, _, _ in quad]
+        elif stage == 3:
             hop = [post(total.at[at.r0], total.at[at.r0], at.core)]
         else:
             hop = []
@@ -280,7 +308,8 @@
     nr, nc = rows // 2, cols // 2
     piece = covar // (4 * nr)
     lshape = (2, nr, 2, piece, rank)
-    hops = 2 * (1 + (nr - 1) + 1) + (nc - 1)
+    quad = 2 * nr - 1
+    hops = 2 * (1 + quad) + (nc - 1)
     smem = pl.BlockSpec(memory_space=pltpu.SMEM)
     return pl.pallas_call(
         functools.partial(field_kernel, rows, cols),
@@ -290,7 +319,7 @@
             jax.ShapeDtypeStruct((slots, block, rank), BF16),
             jax.ShapeDtypeStruct((slots, block, rank), BF16),
         ),
-        in_specs=[smem, smem, VMEM, VMEM, ANY, ANY, ANY, ANY],
+        in_specs=[smem, smem, HBM, HBM, HBM, HBM, HBM, HBM],
         out_specs=(VMEM, VMEM, VMEM, VMEM),
         scratch_shapes=[
             pltpu.VMEM((count, per_device, rank), BF16),
@@ -306,11 +335,11 @@
             pltpu.VMEM(lshape, F32),
             pltpu.VMEM((nr, 2, piece, rank), F32),
             pltpu.VMEM((nr, 2, piece, rank), F32),
-            pltpu.VMEM((nr - 1, 2, piece, rank), F32),
-            pltpu.VMEM((2, piece, rank), F32),
-            pltpu.VMEM((piece, rank), F32),
+            pltpu.VMEM((quad, piece, rank), F32),
             pltpu.VMEM((nc, piece, rank), F32),
-            pltpu.SemaphoreType.DMA((7,)),
+            pltpu.VMEM((per_device, rank), F32),
+            pltpu.VMEM((covar, rank), F32),
+            pltpu.SemaphoreType.DMA((9,)),
             pltpu.SemaphoreType.DMA((count,)),
             pltpu.SemaphoreType.DMA((count,)),
             pltpu.SemaphoreType.DMA((4,)),
@@ -319,7 +348,7 @@
             pltpu.SemaphoreType.DMA((hops,)),
         ],
         compiler_params=pltpu.CompilerParams(
-            collective_id=0, has_side_effects=True, vmem_limit_bytes=LIMIT
+            collective_id=0, has_side_effects=True, vmem_limit_bytes=LIMIT_FIELD
         ),
     )(blocks, live, factors_v, link_beta, covariates, factors_u, noise_u, obs)
 

time: 67.2 us -> 60.9 us (0.906)
  Pallas kernels: 60.1 us -> 53.8 us
    pallas_call x1, Pallas kernels: 40.7 us -> 34.1 us  [run_field(): pl.pallas_call(functools.partial(field_kernel, rows, cols), out_shape=(ja...]
where the time goes in v3:
time: 60.9 us; the launch traced here: 60.6 us
  Pallas kernels  53.8 us (88%)
  local copies, waits for them, and re-layouts  5.53 us (9%)
  between operations  1.32 us (2%)
    pallas_call x1, Pallas kernels, run_field(): pl.pallas_call(functools.partial(field_kernel, rows, cols), out_shape=(ja...  34.1 us
    pallas_call x1, Pallas kernels, run_sum(): pl.pallas_call(functools.partial(sum_kernel, rows, cols, step_day), out_s...  15.9 us
    unnamed x15, local copies, waits for them, and re-layouts  5.53 us
    pallas_call x1, Pallas kernels, run_add(): pl.pallas_call(functools.partial(add_kernel, day_blocks, step_link), out_...  3.84 us

profile of v3, /device:TPU:0, one launch (start us, length us, event | category | flops | bytes accessed | tf_op | source)
XLA Modules:
  0.0 60.6 jit_solution(12359766830045385351)
XLA Ops:
  1.3 0.0 copy-start
  1.3 0.9 %copy-done = f32[512,128]{1,0:T(8,128)S(1)} copy-done((f32[512,128]{1,0:T(8,128)S(1)}, f32[512,128]{1,0:T(8,128)}, u32[]{:S(2)}) %copy-start) | copy-done | bytes 262168
  2.2 0.0 copy-start.1
  2.2 1.2 %copy-done.1 = bf16[32,128,128]{2,1,0:T(8,128)(2,1)S(1)} copy-done((bf16[32,128,128]{2,1,0:T(8,128)(2,1)S(1)}, bf16[32,128,128]{2,1,0:T(8,128)(2,1)}, u32[]{:S(2)}) %copy-start.1) | copy-done | bytes 1048600
  3.5 0.0 copy-start.2
  3.5 1.2 %copy-done.2 = bf16[32,128,128]{2,1,0:T(8,128)(2,1)S(1)} copy-done((bf16[32,128,128]{2,1,0:T(8,128)(2,1)S(1)}, bf16[32,128,128]{2,1,0:T(8,128)(2,1)}, u32[]{:S(2)}) %copy-start.2) | copy-done | bytes 1048600
  4.7 0.0 copy-start.3
  4.7 0.8 %copy-done.3 = f32[128,128]{1,0:T(8,128)S(1)} copy-done((f32[128,128]{1,0:T(8,128)S(1)}, f32[128,128]{1,0:T(8,128)}, u32[]{:S(2)}) %copy-start.3) | copy-done | bytes 65560
  5.5 0.0 copy-start.6
  5.5 0.7 %copy-done.6 = s32[1,128]{1,0:T(1,128)S(1)} copy-done((s32[1,128]{1,0:T(1,128)S(1)}, s32[1,128]{1,0:T(1,128)}, u32[]{:S(2)}) %copy-start.6) | copy-done | bytes 536
  6.2 0.0 copy-start.4
  6.2 34.1 %shard_map.121 = (f32[32,128,128]{2,1,0:T(8,128)S(1)}, f32[2,2,2,64,128]{4,3,2,1,0:T(8,128)S(1)}, bf16[128,128,128]{2,1,0:T(8,128)(2,1)S(1)}, bf16[128,128,128]{2,1,0:T(8,128)(2,1)S(1)}) custom-call(s32[128]{0:T(128)S(1)} %bitcast.6, s32[1]{0:T(128)S(6)} %copy.14.live_ref, f32[128,128]{1,0:T(8,128)S(1)} %copy-done.3, f32[512,128]{1,0:T(8,128)S(1)} %copy-done, ...), custom_call_target="tpu_custom_call" | custom-call | tf_op jit(solution)/shard_map/pallas_call | solution.py:314
  40.2 0.0 copy-done.4
  40.3 0.0 copy-start.5
  40.3 3.8 %shard_map.122 = (bf16[32,128,128]{2,1,0:T(8,128)(2,1)}, bf16[32,128,128]{2,1,0:T(8,128)(2,1)S(1)}, f32[512,128]{1,0:T(8,128)}) custom-call(s32[128]{0:T(128)S(1)} %bitcast.7, f32[32,128,128]{2,1,0:T(8,128)S(1)} %get-tuple-element.10.base_ref, bf16[128,128,128]{2,1,0:T(8,128)(2,1)S(1)} %get-tuple-element.11.grad_ref, ...), custom_call_target="tpu_custom_call" | custom-call | tf_op jit(solution)/shard_map/pallas_call | solution.py:380
  44.1 0.0 copy-done.5
  44.1 15.9 %shard_map.123 = f32[128,128]{1,0:T(8,128)S(1)} custom-call(bf16[2,2,4,2,128,128]{5,4,3,2,1,0:T(8,128)(2,1)S(1)} %bitcast.4, f32[128,128]{1,0:T(8,128)S(1)} %copy-done.3, f32[128,128]{1,0:T(8,128)S(1)} %copy-done.5), custom_call_target="tpu_custom_call" | custom-call | tf_op jit(solution)/shard_map/pallas_call | solution.py:460
  60.0 0.6 %copy.15 = f32[128,128]{1,0:T(8,128)} copy(f32[128,128]{1,0:T(8,128)S(1)} %shard_map.123) | data formatting | bytes 131072
Async XLA Ops:
  1.3 1.0 %copy-start = (f32[512,128]{1,0:T(8,128)S(1)}, f32[512,128]{1,0:T(8,128)}, u32[]{:S(2)}) copy-start(f32[512,128]{1,0:T(8,128)} %beta_ref.3) | copy-start | bytes 786436
  2.2 1.2 %copy-start.1 = (bf16[32,128,128]{2,1,0:T(8,128)(2,1)S(1)}, bf16[32,128,128]{2,1,0:T(8,128)(2,1)}, u32[]{:S(2)}) copy-start(bf16[32,128,128]{2,1,0:T(8,128)(2,1)} %u_hbm.1) | copy-start | bytes 3145732
  3.5 1.2 %copy-start.2 = (bf16[32,128,128]{2,1,0:T(8,128)(2,1)S(1)}, bf16[32,128,128]{2,1,0:T(8,128)(2,1)}, u32[]{:S(2)}) copy-start(bf16[32,128,128]{2,1,0:T(8,128)(2,1)} %nz_hbm.1) | copy-start | bytes 3145732
  4.7 0.8 %copy-start.3 = (f32[128,128]{1,0:T(8,128)S(1)}, f32[128,128]{1,0:T(8,128)}, u32[]{:S(2)}) copy-start(f32[128,128]{1,0:T(8,128)} %fv_ref.3) | copy-start | bytes 196612
  5.5 0.7 %copy-start.6 = (s32[1,128]{1,0:T(1,128)S(1)}, s32[1,128]{1,0:T(1,128)}, u32[]{:S(2)}) copy-start(s32[1,128]{1,0:T(1,128)} %param.15) | copy-start | bytes 1540
  6.2 34.1 %copy-start.4 = (f32[512,128]{1,0:T(8,128)S(1)}, f32[512,128]{1,0:T(8,128)}, u32[]{:S(2)}) copy-start(f32[512,128]{1,0:T(8,128)} %nb_ref.1) | copy-start | bytes 786436
  40.3 3.9 %copy-start.5 = (f32[128,128]{1,0:T(8,128)S(1)}, f32[128,128]{1,0:T(8,128)}, u32[]{:S(2)}) copy-start(f32[128,128]{1,0:T(8,128)} %nv_ref.1) | copy-start | bytes 196612

commit v4 on v3

--- a/solution.py
+++ b/solution.py
@@ -79,7 +79,7 @@
     rows, cols, blocks_ref, live_ref, fv_ref, beta_ref, cov_hbm, u_hbm, nz_hbm, obs_hbm,
     base_ref, total, grad_ref, term_ref,
     days, cov, u, nz, obs, beta, rp, edge_send, edge_recv, link_acc,
-    lk, lk_core, lm_core, lk_quad, lk_z, fv, beta_wide,
+    lk, lk_core, lm_core, lk_quad, lk_z,
     load_sem, day_send, day_recv, halo_send, halo_recv, link_send, link_recv,
 ):
     at = Place(rows, cols)
@@ -92,10 +92,6 @@
         loads.append(pltpu.make_async_copy(cov_hbm.at[pl.ds(k * per, per)], cov.at[pl.ds(k * per, per)], load_sem.at[k]))
     u_load = pltpu.make_async_copy(u_hbm, u, load_sem.at[parts])
     nz_load = pltpu.make_async_copy(nz_hbm, nz, load_sem.at[parts + 1])
-    fv_load = pltpu.make_async_copy(fv_ref, fv, load_sem.at[parts + 3])
-    beta_load = pltpu.make_async_copy(beta_ref, beta_wide, load_sem.at[parts + 4])
-    fv_load.start()
-    beta_load.start()
     loads[0].start()
     u_load.start()
     for load in loads[1:]:
@@ -107,8 +103,7 @@
     def index_of(b):
         return ((b[0] * 2 + b[1]) * nc + b[2]) * 2 + b[3]
 
-    fv_load.wait()
-    days[at.r * cols + at.c] = fv[...].astype(BF16)
+    days[at.r * cols + at.c] = fv_ref[...].astype(BF16)
     north = (lax.rem(at.r + rows - 1, rows), at.c)
     south = (lax.rem(at.r + 1, rows), at.c)
     west = (at.r, lax.rem(at.c + cols - 1, cols))
@@ -142,8 +137,7 @@
     own = (at.r1, at.r0, at.c1, at.c0)
     pass_on(own, zs + [at.side] + xs + [at.core])
 
-    beta_load.wait()
-    beta[...] = beta_wide[...].astype(BF16)
+    beta[...] = beta_ref[...].astype(BF16)
 
     def resid_rows(i):
         cells = cov[pl.ds(i, per)].reshape(per * block, cov.shape[2])
@@ -170,7 +164,7 @@
     for k in range(nc):
         b = (at.r1, at.r0, at.c1_at(nc - k), 1 - at.c0)
         arrive(b)
-        pass_on(b, xs + [at.core])
+        pass_on(b, (xs if k % 2 == 0 else []) + [at.core])
 
     nz_load.wait()
     for halo in halos:
@@ -209,12 +203,6 @@
         else:
             link_acc[...] += prior_rows(k * per)
 
-    for j in range(1, nr):
-        for k in range(nc):
-            for c0 in (at.c0, 1 - at.c0):
-                b = (at.r1_at(nr - j), at.r0, at.c1_at(nc - k), c0)
-                arrive(b)
-                pass_on(b, [at.core])
     lk[...] = link_acc[...].T.reshape(lk.shape)
     used = [0]
     pending = []
@@ -231,6 +219,22 @@
             copy.wait_recv()
 
     hop = [post(lk.at[1 - at.r0], lk_core, at.core)]
+    for j in range(1, nr):
+        for k in range(nc):
+            b = (at.r1_at(nr - j), at.r0, at.c1_at(nc - k), at.c0)
+            arrive(b)
+            pass_on(b, ([at.side] if k % 2 else []) + [at.core])
+    settle(hop)
+    lm_core[...] = lk[at.r0] + lk_core[...]
+    hop = [
+        post(lm_core.at[r1, c0], lk_quad.at[q], device)
+        for q, (device, r1, c0) in enumerate(quad)
+    ]
+    for j in range(1, nr):
+        for k in range(nc):
+            b = (at.r1_at(nr - j), at.r0, at.c1_at(nc - k), 1 - at.c0)
+            arrive(b)
+            pass_on(b, [at.core])
     for j in range(nr):
         for k in range(nc):
             for c0 in (at.c0, 1 - at.c0):
@@ -242,14 +246,14 @@
     span = block // days.shape[1]
     slots = obs.shape[0]
     wide = 16
-    stages = 5
+    stages = 3
     turns = slots // wide
 
     def turn(t, carry):
         taken = []
         for j in range(wide):
             slot = t * wide + j
-            e = blocks_ref[slot]
+            e = blocks_ref[0, slot]
             pb, db = e // day_blocks, lax.rem(e, day_blocks)
             taken.append((slot, u[pb], days[pl.ds(db * span, span)].reshape(block, u.shape[2]), obs[slot]))
         resid = []
@@ -273,25 +277,19 @@
         lax.fori_loop(stage * turns // (stages + 1), (stage + 1) * turns // (stages + 1), turn, 0)
         settle(hop)
         if stage == 0:
-            lm_core[...] = lk[at.r0] + lk_core[...]
-            hop = [
-                post(lm_core.at[r1, c0], lk_quad.at[q], device)
-                for q, (device, r1, c0) in enumerate(quad)
-            ]
-        elif stage == 1:
             link = lm_core[at.r1, at.c0]
             for q in range(len(quad)):
                 link = link + lk_quad[q]
             lk_z[at.c1] = link
             hop = [post(lk_z.at[at.c1], lk_z.at[at.c1], at.z_peer(k)) for k in range(1, nc)]
-        elif stage == 2:
+        elif stage == 1:
             link = lk_z[0]
             for k in range(1, nc):
                 link = link + lk_z[k]
             own_piece = total.at[at.r0, at.r1, at.c0]
             own_piece[...] = link
             hop = [post(own_piece, own_piece, device) for device, _, _ in quad]
-        elif stage == 3:
+        elif stage == 2:
             hop = [post(total.at[at.r0], total.at[at.r0], at.core)]
         else:
             hop = []
@@ -319,7 +317,7 @@
             jax.ShapeDtypeStruct((slots, block, rank), BF16),
             jax.ShapeDtypeStruct((slots, block, rank), BF16),
         ),
-        in_specs=[smem, smem, HBM, HBM, HBM, HBM, HBM, HBM],
+        in_specs=[smem, smem, VMEM, VMEM, HBM, HBM, HBM, HBM],
         out_specs=(VMEM, VMEM, VMEM, VMEM),
         scratch_shapes=[
             pltpu.VMEM((count, per_device, rank), BF16),
@@ -337,9 +335,7 @@
             pltpu.VMEM((nr, 2, piece, rank), F32),
             pltpu.VMEM((quad, piece, rank), F32),
             pltpu.VMEM((nc, piece, rank), F32),
-            pltpu.VMEM((per_device, rank), F32),
-            pltpu.VMEM((covar, rank), F32),
-            pltpu.SemaphoreType.DMA((9,)),
+            pltpu.SemaphoreType.DMA((7,)),
             pltpu.SemaphoreType.DMA((count,)),
             pltpu.SemaphoreType.DMA((count,)),
             pltpu.SemaphoreType.DMA((4,)),
@@ -362,7 +358,7 @@
     def turn(t, carry):
         for j in range(wide):
             slot = t * wide + j
-            e = blocks_ref[slot]
+            e = blocks_ref[0, slot]
             pb, db = e // day_blocks, lax.rem(e, day_blocks)
             acc_u[pb] += 0.5 * step_pixel * grad_ref[slot].astype(F32)
             acc_v[db] += term_ref[slot].astype(F32)
@@ -493,11 +489,11 @@
     step_day = 0.25 / math.sqrt(devices * slots * block / day_blocks)
     step_link = 0.25 / math.sqrt(devices * tile * block)
     base, total, grad, term = run_field(
-        rows, cols, obs_blocks[0], obs_count, factors_v, link_beta, covariates, factors_u, noise_u,
+        rows, cols, obs_blocks, obs_count, factors_v, link_beta, covariates, factors_u, noise_u,
         obs_values[0],
     )
     u_next, dv, beta_next = run_add(
-        day_blocks, step_link, obs_blocks[0], base, grad, term,
+        day_blocks, step_link, obs_blocks, base, grad, term,
         total.reshape(link_beta.shape), link_beta, noise_beta,
     )
     v_next = run_sum(rows, cols, step_day, dv, factors_v, noise_v)

time: 60.9 us -> 59.6 us (0.979)
  Pallas kernels: 53.8 us -> 52.5 us
    pallas_call x1, Pallas kernels: 34.1 us -> 33.1 us  [run_field(): pl.pallas_call(functools.partial(field_kernel, rows, cols), out_shape=(ja...]
where the time goes in v4:
time: 59.6 us; the launch traced here: 59.3 us
  Pallas kernels  52.5 us (88%)
  local copies, waits for them, and re-layouts  5.53 us (9%)
  between operations  1.32 us (2%)
    pallas_call x1, Pallas kernels, run_field(): pl.pallas_call(functools.partial(field_kernel, rows, cols), out_shape=(ja...  33.1 us
    pallas_call x1, Pallas kernels, run_sum(): pl.pallas_call(functools.partial(sum_kernel, rows, cols, step_day), out_s...  15.5 us
    unnamed x15, local copies, waits for them, and re-layouts  5.53 us
    pallas_call x1, Pallas kernels, run_add(): pl.pallas_call(functools.partial(add_kernel, day_blocks, step_link), out_...  3.84 us

profile of v4, /device:TPU:0, one launch (start us, length us, event | category | flops | bytes accessed | tf_op | source)
XLA Modules:
  0.0 59.3 jit_solution(16012221397131995528)
XLA Ops:
  1.3 0.0 copy-start
  1.3 0.9 %copy-done = f32[512,128]{1,0:T(8,128)S(1)} copy-done((f32[512,128]{1,0:T(8,128)S(1)}, f32[512,128]{1,0:T(8,128)}, u32[]{:S(2)}) %copy-start) | copy-done | bytes 262168
  2.2 0.0 copy-start.1
  2.2 1.2 %copy-done.1 = bf16[32,128,128]{2,1,0:T(8,128)(2,1)S(1)} copy-done((bf16[32,128,128]{2,1,0:T(8,128)(2,1)S(1)}, bf16[32,128,128]{2,1,0:T(8,128)(2,1)}, u32[]{:S(2)}) %copy-start.1) | copy-done | bytes 1048600
  3.5 0.0 copy-start.2
  3.5 1.2 %copy-done.2 = bf16[32,128,128]{2,1,0:T(8,128)(2,1)S(1)} copy-done((bf16[32,128,128]{2,1,0:T(8,128)(2,1)S(1)}, bf16[32,128,128]{2,1,0:T(8,128)(2,1)}, u32[]{:S(2)}) %copy-start.2) | copy-done | bytes 1048600
  4.7 0.0 copy-start.3
  4.7 0.8 %copy-done.3 = f32[128,128]{1,0:T(8,128)S(1)} copy-done((f32[128,128]{1,0:T(8,128)S(1)}, f32[128,128]{1,0:T(8,128)}, u32[]{:S(2)}) %copy-start.3) | copy-done | bytes 65560
  5.5 0.0 copy-start.6
  5.5 0.7 %copy-done.6 = s32[1,128]{1,0:T(1,128)S(1)} copy-done((s32[1,128]{1,0:T(1,128)S(1)}, s32[1,128]{1,0:T(1,128)}, u32[]{:S(2)}) %copy-start.6) | copy-done | bytes 536
  6.2 0.0 copy-start.4
  6.2 33.1 %shard_map.121 = (f32[32,128,128]{2,1,0:T(8,128)S(1)}, f32[2,2,2,64,128]{4,3,2,1,0:T(8,128)S(1)}, bf16[128,128,128]{2,1,0:T(8,128)(2,1)S(1)}, bf16[128,128,128]{2,1,0:T(8,128)(2,1)S(1)}) custom-call(s32[1,128]{1,0:T(1,128)S(1)} %copy-done.6, s32[1]{0:T(128)S(6)} %copy.14.live_ref, f32[128,128]{1,0:T(8,128)S(1)} %copy-done.3, f32[512,128]{1,0:T(8,128)S(1)} %copy-done, ...), custom_call_target="tpu_custom_call" | custom-call | tf_op jit(solution)/shard_map/pallas_call | solution.py:312
  39.3 0.0 copy-done.4
  39.3 0.0 copy-start.5
  39.3 3.8 %shard_map.122 = (bf16[32,128,128]{2,1,0:T(8,128)(2,1)}, bf16[32,128,128]{2,1,0:T(8,128)(2,1)S(1)}, f32[512,128]{1,0:T(8,128)}) custom-call(s32[1,128]{1,0:T(1,128)S(1)} %copy-done.6, f32[32,128,128]{2,1,0:T(8,128)S(1)} %get-tuple-element.10.base_ref, bf16[128,128,128]{2,1,0:T(8,128)(2,1)S(1)} %get-tuple-element.11.grad_ref, ...), custom_call_target="tpu_custom_call" | custom-call | tf_op jit(solution)/shard_map/pallas_call | solution.py:376
  43.2 0.0 copy-done.5
  43.2 15.5 %shard_map.123 = f32[128,128]{1,0:T(8,128)S(1)} custom-call(bf16[2,2,4,2,128,128]{5,4,3,2,1,0:T(8,128)(2,1)S(1)} %bitcast.3, f32[128,128]{1,0:T(8,128)S(1)} %copy-done.3, f32[128,128]{1,0:T(8,128)S(1)} %copy-done.5), custom_call_target="tpu_custom_call" | custom-call | tf_op jit(solution)/shard_map/pallas_call | solution.py:456
  58.7 0.6 %copy.15 = f32[128,128]{1,0:T(8,128)} copy(f32[128,128]{1,0:T(8,128)S(1)} %shard_map.123) | data formatting | bytes 131072
Async XLA Ops:
  1.3 1.0 %copy-start = (f32[512,128]{1,0:T(8,128)S(1)}, f32[512,128]{1,0:T(8,128)}, u32[]{:S(2)}) copy-start(f32[512,128]{1,0:T(8,128)} %beta_ref.3) | copy-start | bytes 786436
  2.2 1.2 %copy-start.1 = (bf16[32,128,128]{2,1,0:T(8,128)(2,1)S(1)}, bf16[32,128,128]{2,1,0:T(8,128)(2,1)}, u32[]{:S(2)}) copy-start(bf16[32,128,128]{2,1,0:T(8,128)(2,1)} %u_hbm.1) | copy-start | bytes 3145732
  3.5 1.2 %copy-start.2 = (bf16[32,128,128]{2,1,0:T(8,128)(2,1)S(1)}, bf16[32,128,128]{2,1,0:T(8,128)(2,1)}, u32[]{:S(2)}) copy-start(bf16[32,128,128]{2,1,0:T(8,128)(2,1)} %nz_hbm.1) | copy-start | bytes 3145732
  4.7 0.8 %copy-start.3 = (f32[128,128]{1,0:T(8,128)S(1)}, f32[128,128]{1,0:T(8,128)}, u32[]{:S(2)}) copy-start(f32[128,128]{1,0:T(8,128)} %fv_ref.3) | copy-start | bytes 196612
  5.5 0.7 %copy-start.6 = (s32[1,128]{1,0:T(1,128)S(1)}, s32[1,128]{1,0:T(1,128)}, u32[]{:S(2)}) copy-start(s32[1,128]{1,0:T(1,128)} %blocks_ref.3) | copy-start | bytes 1540
  6.2 33.1 %copy-start.4 = (f32[512,128]{1,0:T(8,128)S(1)}, f32[512,128]{1,0:T(8,128)}, u32[]{:S(2)}) copy-start(f32[512,128]{1,0:T(8,128)} %nb_ref.1) | copy-start | bytes 786436
  39.3 3.9 %copy-start.5 = (f32[128,128]{1,0:T(8,128)S(1)}, f32[128,128]{1,0:T(8,128)}, u32[]{:S(2)}) copy-start(f32[128,128]{1,0:T(8,128)} %nv_ref.1) | copy-start | bytes 196612

commit v5 on v4

--- a/solution.py
+++ b/solution.py
@@ -76,9 +76,9 @@
 
 
 def field_kernel(
-    rows, cols, blocks_ref, live_ref, fv_ref, beta_ref, cov_hbm, u_hbm, nz_hbm, obs_hbm,
+    rows, cols, blocks_ref, live_ref, fv_ref, beta_ref, cov_hbm, u_hbm, obs_hbm,
     base_ref, total, grad_ref, term_ref,
-    days, cov, u, nz, obs, beta, rp, edge_send, edge_recv, link_acc,
+    days, cov, u, obs, beta, rp, edge_send, edge_recv, link_acc,
     lk, lk_core, lm_core, lk_quad, lk_z,
     load_sem, day_send, day_recv, halo_send, halo_recv, link_send, link_recv,
 ):
@@ -91,13 +91,11 @@
     for k in range(parts):
         loads.append(pltpu.make_async_copy(cov_hbm.at[pl.ds(k * per, per)], cov.at[pl.ds(k * per, per)], load_sem.at[k]))
     u_load = pltpu.make_async_copy(u_hbm, u, load_sem.at[parts])
-    nz_load = pltpu.make_async_copy(nz_hbm, nz, load_sem.at[parts + 1])
     loads[0].start()
     u_load.start()
     for load in loads[1:]:
         load.start()
-    nz_load.start()
-    obs_load = pltpu.make_async_copy(obs_hbm, obs, load_sem.at[parts + 2])
+    obs_load = pltpu.make_async_copy(obs_hbm, obs, load_sem.at[parts + 1])
     obs_load.start()
 
     def index_of(b):
@@ -166,7 +164,6 @@
         arrive(b)
         pass_on(b, (xs if k % 2 == 0 else []) + [at.core])
 
-    nz_load.wait()
     for halo in halos:
         halo.wait()
     for spot, gone in ((0, at.r == 0), (tile + 1, at.r == rows - 1)):
@@ -188,7 +185,6 @@
         base_ref[pl.ds(i, per)] = (
             u[pl.ds(i, per)].astype(F32)
             - 0.5 * step_pixel * prior
-            + math.sqrt(step_pixel) * nz[pl.ds(i, per)].astype(F32)
         )
         return lax.dot_general(
             prior.astype(BF16).reshape(per * block, -1),
@@ -297,7 +293,7 @@
         copy.wait_send()
 
 
-def run_field(rows, cols, blocks, live, factors_v, link_beta, covariates, factors_u, noise_u, obs):
+def run_field(rows, cols, blocks, live, factors_v, link_beta, covariates, factors_u, obs):
     tile, block, rank = factors_u.shape
     covar = covariates.shape[2]
     per_device = factors_v.shape[0]
@@ -317,12 +313,11 @@
             jax.ShapeDtypeStruct((slots, block, rank), BF16),
             jax.ShapeDtypeStruct((slots, block, rank), BF16),
         ),
-        in_specs=[smem, smem, VMEM, VMEM, HBM, HBM, HBM, HBM],
+        in_specs=[smem, smem, VMEM, VMEM, HBM, HBM, HBM],
         out_specs=(VMEM, VMEM, VMEM, VMEM),
         scratch_shapes=[
             pltpu.VMEM((count, per_device, rank), BF16),
             pltpu.VMEM((tile, block, covar), BF16),
-            pltpu.VMEM((tile, block, rank), BF16),
             pltpu.VMEM((tile, block, rank), BF16),
             pltpu.VMEM((slots, block, block), BF16),
             pltpu.VMEM((covar, rank), BF16),
@@ -335,7 +330,7 @@
             pltpu.VMEM((nr, 2, piece, rank), F32),
             pltpu.VMEM((quad, piece, rank), F32),
             pltpu.VMEM((nc, piece, rank), F32),
-            pltpu.SemaphoreType.DMA((7,)),
+            pltpu.SemaphoreType.DMA((6,)),
             pltpu.SemaphoreType.DMA((count,)),
             pltpu.SemaphoreType.DMA((count,)),
             pltpu.SemaphoreType.DMA((4,)),
@@ -346,12 +341,12 @@
         compiler_params=pltpu.CompilerParams(
             collective_id=0, has_side_effects=True, vmem_limit_bytes=LIMIT_FIELD
         ),
-    )(blocks, live, factors_v, link_beta, covariates, factors_u, noise_u, obs)
-
-
-def add_kernel(day_blocks, step_link, blocks_ref, base_ref, grad_ref, term_ref, total_ref, beta_ref, nb_ref,
+    )(blocks, live, factors_v, link_beta, covariates, factors_u, obs)
+
+
+def add_kernel(day_blocks, step_link, blocks_ref, base_ref, nz_ref, grad_ref, term_ref, total_ref, beta_ref, nb_ref,
                next_ref, dv_ref, beta_out, acc_u, acc_v):
-    acc_u[...] = base_ref[...]
+    acc_u[...] = base_ref[...] + math.sqrt(step_pixel) * nz_ref[...].astype(F32)
     acc_v[...] = jnp.zeros_like(acc_v)
     wide = 4
 
@@ -371,7 +366,7 @@
     beta_out[...] = old + 0.5 * step_link * (total_ref[...] - old) + math.sqrt(step_link) * nb_ref[...]
 
 
-def run_add(day_blocks, step_link, blocks, base, grad, term, total, link_beta, noise_beta):
+def run_add(day_blocks, step_link, blocks, base, noise_u, grad, term, total, link_beta, noise_beta):
     tile, block, rank = base.shape
     return pl.pallas_call(
         functools.partial(add_kernel, day_blocks, step_link),
@@ -380,14 +375,14 @@
             jax.ShapeDtypeStruct((day_blocks, block, rank), BF16),
             jax.ShapeDtypeStruct(link_beta.shape, F32),
         ),
-        in_specs=[pl.BlockSpec(memory_space=pltpu.SMEM)] + [VMEM] * 6,
+        in_specs=[pl.BlockSpec(memory_space=pltpu.SMEM)] + [VMEM] * 7,
         out_specs=(VMEM, VMEM, VMEM),
         scratch_shapes=[
             pltpu.VMEM((tile, block, rank), F32),
             pltpu.VMEM((day_blocks, block, rank), F32),
         ],
         compiler_params=pltpu.CompilerParams(vmem_limit_bytes=LIMIT),
-    )(blocks, base, grad, term, total, link_beta, noise_beta)
+    )(blocks, base, noise_u, grad, term, total, link_beta, noise_beta)
 
 
 def sum_kernel(
@@ -489,11 +484,10 @@
     step_day = 0.25 / math.sqrt(devices * slots * block / day_blocks)
     step_link = 0.25 / math.sqrt(devices * tile * block)
     base, total, grad, term = run_field(
-        rows, cols, obs_blocks, obs_count, factors_v, link_beta, covariates, factors_u, noise_u,
-        obs_values[0],
+        rows, cols, obs_blocks, obs_count, factors_v, link_beta, covariates, factors_u, obs_values[0],
     )
     u_next, dv, beta_next = run_add(
-        day_blocks, step_link, obs_blocks, base, grad, term,
+        day_blocks, step_link, obs_blocks, base, noise_u, grad, term,
         total.reshape(link_beta.shape), link_beta, noise_beta,
     )
     v_next = run_sum(rows, cols, step_day, dv, factors_v, noise_v)

time: 59.6 us -> 58.2 us (0.977)
  local copies, waits for them, and re-layouts: 5.53 us -> 4.31 us
    unnamed x15, local copies, waits for them, and re-layouts: 5.53 us -> 4.31 us
where the time goes in v5:
time: 58.2 us; the launch traced here: 58 us
  Pallas kernels  52.3 us (90%)
  local copies, waits for them, and re-layouts  4.31 us (7%)
  between operations  1.33 us (2%)
    pallas_call x1, Pallas kernels, run_field(): pl.pallas_call(functools.partial(field_kernel, rows, cols), out_shape=(ja...  32.9 us
    pallas_call x1, Pallas kernels, run_sum(): pl.pallas_call(functools.partial(sum_kernel, rows, cols, step_day), out_s...  15.5 us
    unnamed x15, local copies, waits for them, and re-layouts  4.31 us
    pallas_call x1, Pallas kernels, run_add(): pl.pallas_call(functools.partial(add_kernel, day_blocks, step_link), out_...  3.93 us

profile of v5, /device:TPU:0, one launch (start us, length us, event | category | flops | bytes accessed | tf_op | source)
XLA Modules:
  0.0 58.0 jit_solution(7393485663498015705)
XLA Ops:
  1.3 0.0 copy-start
  1.3 1.2 %copy-done = bf16[32,128,128]{2,1,0:T(8,128)(2,1)S(1)} copy-done((bf16[32,128,128]{2,1,0:T(8,128)(2,1)S(1)}, bf16[32,128,128]{2,1,0:T(8,128)(2,1)}, u32[]{:S(2)}) %copy-start) | copy-done | bytes 1048600
  2.5 0.0 copy-start.2
  2.5 0.9 %copy-done.2 = f32[512,128]{1,0:T(8,128)S(1)} copy-done((f32[512,128]{1,0:T(8,128)S(1)}, f32[512,128]{1,0:T(8,128)}, u32[]{:S(2)}) %copy-start.2) | copy-done | bytes 262168
  3.5 0.0 copy-start.3
  3.5 0.8 %copy-done.3 = f32[128,128]{1,0:T(8,128)S(1)} copy-done((f32[128,128]{1,0:T(8,128)S(1)}, f32[128,128]{1,0:T(8,128)}, u32[]{:S(2)}) %copy-start.3) | copy-done | bytes 65560
  4.3 0.0 copy-start.6
  4.3 0.7 %copy-done.6 = s32[1,128]{1,0:T(1,128)S(1)} copy-done((s32[1,128]{1,0:T(1,128)S(1)}, s32[1,128]{1,0:T(1,128)}, u32[]{:S(2)}) %copy-start.6) | copy-done | bytes 536
  5.0 0.0 copy-start.1
  5.0 0.0 copy-start.4
  5.0 32.9 %shard_map.121 = (f32[32,128,128]{2,1,0:T(8,128)S(1)}, f32[2,2,2,64,128]{4,3,2,1,0:T(8,128)S(1)}, bf16[128,128,128]{2,1,0:T(8,128)(2,1)S(1)}, bf16[128,128,128]{2,1,0:T(8,128)(2,1)S(1)}) custom-call(s32[1,128]{1,0:T(1,128)S(1)} %copy-done.6, s32[1]{0:T(128)S(6)} %copy.14.live_ref, f32[128,128]{1,0:T(8,128)S(1)} %copy-done.3, f32[512,128]{1,0:T(8,128)S(1)} %copy-done.2, ...), custom_call_target="tpu_custom_call" | custom-call | tf_op jit(solution)/shard_map/pallas_call | solution.py:308
  37.9 0.0 copy-done.1
  37.9 0.0 copy-done.4
  37.9 0.0 copy-start.5
  37.9 3.9 %shard_map.122 = (bf16[32,128,128]{2,1,0:T(8,128)(2,1)}, bf16[32,128,128]{2,1,0:T(8,128)(2,1)S(1)}, f32[512,128]{1,0:T(8,128)}) custom-call(s32[1,128]{1,0:T(1,128)S(1)} %copy-done.6, f32[32,128,128]{2,1,0:T(8,128)S(1)} %get-tuple-element.10.base_ref, bf16[32,128,128]{2,1,0:T(8,128)(2,1)S(1)} %copy-done.1, ...), custom_call_target="tpu_custom_call" | custom-call | tf_op jit(solution)/shard_map/pallas_call | solution.py:371
  41.8 0.0 copy-done.5
  41.8 15.5 %shard_map.123 = f32[128,128]{1,0:T(8,128)S(1)} custom-call(bf16[2,2,4,2,128,128]{5,4,3,2,1,0:T(8,128)(2,1)S(1)} %bitcast.3, f32[128,128]{1,0:T(8,128)S(1)} %copy-done.3, f32[128,128]{1,0:T(8,128)S(1)} %copy-done.5), custom_call_target="tpu_custom_call" | custom-call | tf_op jit(solution)/shard_map/pallas_call | solution.py:451
  57.4 0.6 %copy.15 = f32[128,128]{1,0:T(8,128)} copy(f32[128,128]{1,0:T(8,128)S(1)} %shard_map.123) | data formatting | bytes 131072
Async XLA Ops:
  1.3 1.2 %copy-start = (bf16[32,128,128]{2,1,0:T(8,128)(2,1)S(1)}, bf16[32,128,128]{2,1,0:T(8,128)(2,1)}, u32[]{:S(2)}) copy-start(bf16[32,128,128]{2,1,0:T(8,128)(2,1)} %u_hbm.1) | copy-start | bytes 3145732
  2.5 0.9 %copy-start.2 = (f32[512,128]{1,0:T(8,128)S(1)}, f32[512,128]{1,0:T(8,128)}, u32[]{:S(2)}) copy-start(f32[512,128]{1,0:T(8,128)} %beta_ref.3) | copy-start | bytes 786436
  3.5 0.8 %copy-start.3 = (f32[128,128]{1,0:T(8,128)S(1)}, f32[128,128]{1,0:T(8,128)}, u32[]{:S(2)}) copy-start(f32[128,128]{1,0:T(8,128)} %fv_ref.3) | copy-start | bytes 196612
  4.3 0.7 %copy-start.6 = (s32[1,128]{1,0:T(1,128)S(1)}, s32[1,128]{1,0:T(1,128)}, u32[]{:S(2)}) copy-start(s32[1,128]{1,0:T(1,128)} %blocks_ref.3) | copy-start | bytes 1540
  5.0 32.9 %copy-start.1 = (bf16[32,128,128]{2,1,0:T(8,128)(2,1)S(1)}, bf16[32,128,128]{2,1,0:T(8,128)(2,1)}, u32[]{:S(2)}) copy-start(bf16[32,128,128]{2,1,0:T(8,128)(2,1)} %nz_ref.1) | copy-start | bytes 3145732
  5.0 32.9 %copy-start.4 = (f32[512,128]{1,0:T(8,128)S(1)}, f32[512,128]{1,0:T(8,128)}, u32[]{:S(2)}) copy-start(f32[512,128]{1,0:T(8,128)} %nb_ref.1) | copy-start | bytes 786436
  37.9 3.9 %copy-start.5 = (f32[128,128]{1,0:T(8,128)S(1)}, f32[128,128]{1,0:T(8,128)}, u32[]{:S(2)}) copy-start(f32[128,128]{1,0:T(8,128)} %nv_ref.1) | copy-start | bytes 196612
